TPU v7x, 32 devices: a whole 2x2x4 slice. The times are simulated.
32 devices in a mesh: heads: 2 (over x), pages: 16 (over z, y, core).
Axes of the slice: x: 2, y: 2, z: 4, core: 2. Of those that a mesh axis runs over, the one named last changes fastest.
Arguments:
- queries: bfloat16 [4608, 16, 128], P('pages', 'heads'), may hold values from -60 to 60
- keys: bfloat16 [4608, 16, 128], P('pages', 'heads'), may hold values from -6 to 6
- values: bfloat16 [4608, 16, 128], P('pages', 'heads'), may hold values from -6 to 6
- key_cache: bfloat16 [192, 128, 16, 128], P('pages', None, 'heads'), may hold values from -6 to 6
- value_cache: bfloat16 [192, 128, 16, 128], P('pages', None, 'heads'), may hold values from -6 to 6
- cache_len: int32 [6], replicated, may hold values from 0 to 3328, as said below
- page_table: int32 [6, 26], replicated, may hold values from 0 to 191, as said below
- append_slots: int32 [6, 6], replicated, may hold values from 0 to 191
- out_weight: bfloat16 [2048, 4096], P('heads', 'pages'), may hold values from -0.125 to 0.125
- out_bias: float32 [4096], P('heads'), may hold values from -3 to 3
Outputs:
- hidden: bfloat16 [4608, 4096], P('pages', 'heads')
- key_cache_out: bfloat16 [192, 128, 16, 128], P('pages', None, 'heads')
- value_cache_out: bfloat16 [192, 128, 16, 128], P('pages', None, 'heads')
Inputs may be any that keep to these rules, and one draw needn't show every extreme that they name: Every entry of page_table and append_slots together is a different slot. `cache_len`: A multiple of 128; some request has exactly 3328.
All inputs are finite; a program needn't handle non-finite values.
Results may differ from a plain program's by a relative error of at most 0.018.
Values may be sent and summed in bfloat16 or wider, within the bound.
No kernel may reach another device: no remote copies, remote signals or barrier semaphores. Data moves between devices by JAX's collectives and lax.ppermute only.
A program may use at most 128 MiB of HBM per device.

v0:
```python
import functools
import math

import jax
import jax.numpy as jnp
from jax import lax
from jax.experimental import pallas as pl
from jax.experimental.layout import Layout, with_layout_constraint
from jax.experimental.pallas import tpu as pltpu
from jax.sharding import PartitionSpec as P

ROT = 32
PAGE = 128
QTILE = 256

low_score = -(2.0**99)


def rotate(vectors, positions):
    half_rot = ROT // 2
    inv_freq = 10000.0 ** (-2.0 * jnp.arange(half_rot, dtype=jnp.float32) / ROT)
    angles = positions[:, None] * inv_freq[None, :]
    cosine = jnp.cos(angles)[:, None, :]
    sine = jnp.sin(angles)[:, None, :]
    first_half = vectors[..., :half_rot]
    second_half = vectors[..., half_rot:ROT]
    return jnp.concatenate(
        [
            first_half * cosine - second_half * sine,
            second_half * cosine + first_half * sine,
            vectors[..., ROT:],
        ],
        axis=-1,
    )


def stat_rows_of(part_len, unit):
    per_unit = -(-unit // 128)
    units = part_len // unit
    return per_unit, units, -(-3 * units * per_unit // 16) * 16


def stat_rows(row):
    unit = row.shape[1]
    full = -(-unit // 128) * 128
    if full > unit:
        row = jnp.concatenate([row, jnp.zeros((1, full - unit), row.dtype)], axis=1)
    return [row[:, at : at + 128] for at in range(0, full, 128)]


def stat_block(kinds, pad_to):
    rows = [piece for kind in kinds for row in kind for piece in stat_rows(row)]
    rows.append(jnp.zeros((pad_to - len(rows), 128), jnp.float32))
    return jnp.concatenate(rows, axis=0).astype(jnp.bfloat16)


def cached_kernel(unit, span, scale2, places, at_ref, ok_ref, order_ref, start_ref, count_ref,
                  *refs):
    q_refs, (k_ref, v_ref), refs = refs[:places], refs[places : places + 2], refs[places + 2 :]
    o_refs, (q_all, o_all, s_all, q_scr, m_scr, l_scr, acc_scr) = refs[:-7], refs[-7:]
    requests = count_ref.shape[0]
    chips, part_len, _ = q_all.shape
    per_part = part_len // unit
    per_request = span // unit
    per_unit, _, pad_to = stat_rows_of(part_len, unit)

    for index in range(places):

        @pl.when(ok_ref[index] > 0)
        def _(index=index):
            q_all[at_ref[index]] = q_refs[index][0]

    def place(request, index):
        at = request * per_request + index
        return at // per_part, at % per_part

    def one_request(request, _):
        for index in range(per_request):
            part, piece = place(request, index)
            row = pl.ds(pl.multiple_of(piece * unit, unit), unit)
            q_scr[index * unit : (index + 1) * unit, :] = q_all[part, row, :]
        first = start_ref[request]
        count = count_ref[request]
        m_scr[...] = jnp.full((1, span), low_score, jnp.float32)
        l_scr[...] = jnp.zeros((1, span), jnp.float32)
        acc_scr[...] = jnp.zeros(acc_scr.shape, jnp.float32)

        def pages(slots):
            k = jnp.concatenate([k_ref[0, s] for s in slots], axis=0)
            v = jnp.concatenate([v_ref[0, s] for s in slots], axis=1)
            for c in range(0, span, QTILE):
                cols = slice(c, c + QTILE)
                scores = lax.dot_general(
                    k, q_scr[cols, :], (((1,), (1,)), ((), ())),
                    preferred_element_type=jnp.float32,
                )
                before = m_scr[:, cols]
                peak = jnp.maximum(before, jnp.max(scores, axis=0, keepdims=True))
                weights = jnp.exp2((scores - peak) * scale2)
                fade = jnp.exp2((before - peak) * scale2)
                m_scr[:, cols] = peak
                l_scr[:, cols] = l_scr[:, cols] * fade + jnp.sum(weights, axis=0, keepdims=True)
                acc_scr[:, cols] = acc_scr[:, cols] * fade + jnp.dot(
                    v, weights.astype(jnp.bfloat16), preferred_element_type=jnp.float32
                )

        def pair(index, _):
            at = first + 2 * index
            pages([order_ref[at], order_ref[at + 1]])
            return 0

        lax.fori_loop(0, count // 2, pair, 0)

        @pl.when(count % 2 == 1)
        def _():
            pages([order_ref[first + count - 1]])

        totals = l_scr[...]
        peaks = m_scr[...]
        out = (acc_scr[...] / jnp.maximum(totals, 1e-30)).T.astype(jnp.bfloat16)
        sent = peaks.astype(jnp.bfloat16).astype(jnp.float32)
        totals = totals * jnp.exp2((peaks - sent) * scale2)
        high = totals.astype(jnp.bfloat16).astype(jnp.float32)
        kinds = [sent, high, totals - high]
        for index in range(per_request):
            part, piece = place(request, index)
            cols = slice(index * unit, (index + 1) * unit)
            row = pl.ds(pl.multiple_of(piece * unit, unit), unit)
            o_all[part, row, :] = out[cols, :]
            for kind, values in enumerate(kinds):
                for r, line in enumerate(stat_rows(values[:, cols])):
                    at = (kind * per_part + piece) * per_unit + r
                    s_all[part, pl.ds(at, 1), :] = line
        return 0

    lax.fori_loop(0, requests, one_request, 0)
    for index in range(chips):
        part = at_ref[places + index]
        o_refs[index][0, :part_len, :] = o_all[part]
        o_refs[index][0, part_len:, :] = s_all[part].astype(jnp.bfloat16)


def cached_attention(q_places, at, ok, out_at, k_heads, v_heads, order, starts, counts, span,
                     scale2):
    places = len(q_places)
    chips = len(out_at)
    heads, part_len, head_dim = q_places[0].shape
    slots = k_heads.shape[1]
    unit = math.gcd(span, part_len)
    _, _, pad_to = stat_rows_of(part_len, unit)
    own_block = lambda *dims: pl.BlockSpec(
        (1,) + dims, lambda h, *_: (h,) + (0,) * len(dims)
    )
    return pl.pallas_call(
        lambda *refs: cached_kernel(unit, span, scale2, places, *refs),
        grid_spec=pltpu.PrefetchScalarGridSpec(
            num_scalar_prefetch=5,
            grid=(heads,),
            in_specs=[own_block(part_len, head_dim)] * places
            + [own_block(slots, PAGE, head_dim), own_block(slots, head_dim, PAGE)],
            out_specs=[own_block(part_len + pad_to, head_dim)] * chips,
            scratch_shapes=[
                pltpu.VMEM((chips, part_len, head_dim), jnp.bfloat16),
                pltpu.VMEM((chips, part_len, head_dim), jnp.bfloat16),
                pltpu.VMEM((chips, pad_to, 128), jnp.float32),
                pltpu.VMEM((span, head_dim), jnp.bfloat16),
                pltpu.VMEM((1, span), jnp.float32),
                pltpu.VMEM((1, span), jnp.float32),
                pltpu.VMEM((head_dim, span), jnp.float32),
            ],
        ),
        out_shape=[
            jax.ShapeDtypeStruct((heads, part_len + pad_to, head_dim), jnp.bfloat16)
        ] * chips,
        compiler_params=pltpu.CompilerParams(vmem_limit_bytes=40 * 2**20),
        name="cached_attention",
    )(jnp.stack(at + out_at), jnp.stack(ok), order, starts, counts, *q_places, k_heads, v_heads)


def merge_kernel(unit, part_len, scale2, ok_ref, *refs):
    in_refs, out_ref = refs[:-1], refs[-1]
    head_dim = out_ref.shape[2]
    per_unit, units, pad_to = stat_rows_of(part_len, unit)
    stats = [ref[0, part_len:, :].astype(jnp.float32) for ref in in_refs]
    kinds = [[], [], []]
    for u in range(units):

        def line(stat, kind):
            at = (kind * units + u) * per_unit
            pieces = [stat[at + r : at + r + 1, :] for r in range(per_unit)]
            return jnp.concatenate(pieces, axis=1)

        peaks, totals = [], []
        for index, stat in enumerate(stats):
            ok = ok_ref[index] > 0
            peaks.append(jnp.where(ok, line(stat, 0), low_score))
            totals.append(jnp.where(ok, line(stat, 1) + line(stat, 2), 0.0))
        top = functools.reduce(jnp.maximum, peaks)
        shares = [t * jnp.exp2((p - top) * scale2) for t, p in zip(totals, peaks)]
        total = functools.reduce(jnp.add, shares)
        inverse = 1.0 / jnp.maximum(total, 1e-30)
        rows = slice(u * unit, (u + 1) * unit)
        merged = None
        for ref, share in zip(in_refs, shares):
            part = jnp.broadcast_to(share * inverse, (head_dim, share.shape[1])).T[:unit]
            part = part * ref[0, rows, :].astype(jnp.float32)
            merged = part if merged is None else merged + part
        out_ref[0, rows, :] = merged.astype(jnp.bfloat16)
        high = total.astype(jnp.bfloat16).astype(jnp.float32)
        for kind, value in zip(kinds, (top, high, total - high)):
            kind.append(value)
    out_ref[0, part_len:, :] = stat_block(kinds, pad_to)


def merge(parts, ok, part_len, unit, scale2):
    block = pl.BlockSpec((1,) + parts[0].shape[1:], lambda h, *_: (h, 0, 0))
    return pl.pallas_call(
        lambda *refs: merge_kernel(unit, part_len, scale2, *refs),
        grid_spec=pltpu.PrefetchScalarGridSpec(
            num_scalar_prefetch=1,
            grid=(parts[0].shape[0],),
            in_specs=[block] * len(parts),
            out_specs=block,
        ),
        out_shape=jax.ShapeDtypeStruct(parts[0].shape, jnp.bfloat16),
        name="merge",
    )(jnp.stack(ok).astype(jnp.int32), *parts)


def page_kernel(fresh_ref, index_ref, kc_ref, vc_ref, kn_ref, vn_ref, ko_ref, vo_ref):
    fresh = fresh_ref[pl.program_id(0)] > 0

    @pl.when(fresh)
    def _():
        ko_ref[...] = kn_ref[...]
        vo_ref[...] = vn_ref[...]

    @pl.when(jnp.logical_not(fresh))
    def _():
        ko_ref[...] = kc_ref[...]
        vo_ref[...] = vc_ref[...]


def write_pages(key_cache, value_cache, new_keys, new_values, is_fresh, fresh_index):
    block = (1,) + key_cache.shape[1:]
    own = pl.BlockSpec(block, lambda s, fresh, index: (s, 0, 0, 0))
    new = pl.BlockSpec(block, lambda s, fresh, index: (index[s], 0, 0, 0))
    return pl.pallas_call(
        page_kernel,
        grid_spec=pltpu.PrefetchScalarGridSpec(
            num_scalar_prefetch=2,
            grid=(key_cache.shape[0],),
            in_specs=[own, own, new, new],
            out_specs=[own, own],
        ),
        out_shape=[jax.ShapeDtypeStruct(key_cache.shape, key_cache.dtype)] * 2,
        compiler_params=pltpu.CompilerParams(vmem_limit_bytes=40 * 2**20),
        name="write_pages",
    )(is_fresh.astype(jnp.int32), fresh_index, key_cache, value_cache, new_keys, new_values)


def swap(x, bit):
    devs = lax.axis_size("pages")
    return lax.ppermute(x, "pages", [(p, p ^ bit) for p in range(devs)])


def shift(x, hop, senders):
    devs = lax.axis_size("pages")
    moves = [(p, p + 4 * hop) for p in range(devs) if p // 4 in senders]
    return lax.ppermute(x, "pages", moves)


def gather_lines(x):
    line = lax.axis_size("pages") // 4
    device_at = lax.axis_index("pages")
    at, across = device_at // 4, (device_at // 2) % 2
    always = jnp.int32(1)
    held = [(x, at, across, always), (swap(x, 2), at, 1 - across, always)]
    up = down = x
    for t in range(1, line):
        up = shift(up, 1, range(t - 1, line - 1))
        down = shift(down, -1, range(1, line - t + 1))
        has_up = (at >= t).astype(jnp.int32)
        has_down = (at + t < line).astype(jnp.int32)
        devs = lax.axis_size("pages")
        cross_up = [(p, p ^ 2) for p in range(devs) if p // 4 >= t]
        cross_down = [(p, p ^ 2) for p in range(devs) if p // 4 + t < line]
        held += [
            (up, at - t, across, has_up),
            (lax.ppermute(up, "pages", cross_up), at - t, 1 - across, has_up),
            (down, at + t, across, has_down),
            (lax.ppermute(down, "pages", cross_down), at + t, 1 - across, has_down),
        ]
    return held


def merge_lines(parts, merged):
    line = lax.axis_size("pages") // 4
    at = lax.axis_index("pages") // 4
    turns = []
    for t in range(1, line):
        turns += [k for k in (line - t, t) if k not in turns]
    yes = jnp.int32(1)
    crossed = {k: swap(parts[k][1], 2) for k in turns + [0]}
    shares = {}

    def share(k):
        if k not in shares:
            shares[k] = merged([parts[k][0], crossed[k]], [yes, yes])
        return shares[k]

    up = down = None
    for t in range(1, line):
        up_out, down_out = share(line - t), share(t)
        if up is not None:
            up_out = merged([up_out, up], [yes, (at >= 1) & (at <= t - 1)])
            down_out = merged([down_out, down], [yes, (at <= line - 2) & (at >= line - t)])
        up = shift(up_out, 1, range(0, t))
        down = shift(down_out, -1, range(line - t, line))
    return merged([share(0), up, down], [yes, at >= 1, at <= line - 2])


def fresh_kernel(scale2, q_ref, k_ref, v_ref, tok_ref, key_ref, o_ref, m_ref, l_ref):
    scores = lax.dot_general(
        k_ref[0], q_ref[0], (((1,), (1,)), ((), ())), preferred_element_type=jnp.float32
    )
    token = tok_ref[0:1, :]
    first = tok_ref[1:2, :]
    key = key_ref[:, 0:1]
    visible = (key <= token) & (key >= first)
    scores = jnp.where(visible, scores, low_score)
    peak = jnp.max(scores, axis=0, keepdims=True)
    weights = jnp.where(visible, jnp.exp2((scores - peak) * scale2), 0.0)
    m_ref[0] = peak
    l_ref[0] = jnp.sum(weights, axis=0, keepdims=True)
    o_ref[0] = jnp.dot(
        v_ref[0], weights.astype(jnp.bfloat16), preferred_element_type=jnp.float32
    )


def fresh_attention(q_own, k_window, v_window, token_rows, key_cols, scale2):
    heads, tok_dev, head_dim = q_own.shape
    window = k_window.shape[1]
    own = lambda h: (h, 0, 0)
    fixed = lambda h: (0, 0)
    return pl.pallas_call(
        lambda *refs: fresh_kernel(scale2, *refs),
        grid=(heads,),
        in_specs=[
            pl.BlockSpec((1, tok_dev, head_dim), own),
            pl.BlockSpec((1, window, head_dim), own),
            pl.BlockSpec((1, head_dim, window), own),
            pl.BlockSpec(token_rows.shape, fixed),
            pl.BlockSpec(key_cols.shape, fixed),
        ],
        out_specs=[
            pl.BlockSpec((1, head_dim, tok_dev), own),
            pl.BlockSpec((1, 1, tok_dev), own),
            pl.BlockSpec((1, 1, tok_dev), own),
        ],
        out_shape=[
            jax.ShapeDtypeStruct((heads, head_dim, tok_dev), jnp.float32),
            jax.ShapeDtypeStruct((heads, 1, tok_dev), jnp.float32),
            jax.ShapeDtypeStruct((heads, 1, tok_dev), jnp.float32),
        ],
        compiler_params=pltpu.CompilerParams(vmem_limit_bytes=40 * 2**20),
        name="fresh_attention",
    )(q_own, k_window, v_window, token_rows, key_cols)


def per_device(
    queries,
    keys,
    values,
    key_cache,
    value_cache,
    cache_len,
    page_table,
    append_slots,
    out_weight,
    out_bias,
):
    tok_dev, head_count, head_dim = queries.shape
    requests = cache_len.shape[0]
    max_pages = page_table.shape[1]
    new_pages = append_slots.shape[1]
    span_len = new_pages * PAGE
    slot_count = key_cache.shape[0]
    tokens = requests * span_len
    page_devs = tokens // tok_dev
    scale2 = math.log2(math.e) / math.sqrt(head_dim)
    device_at = lax.axis_index("pages")
    token_ids = device_at * tok_dev + jnp.arange(tok_dev, dtype=jnp.int32)
    request_ids = token_ids // span_len
    request_grid = jnp.arange(requests, dtype=jnp.int32)
    starts = jnp.sum(
        jnp.where(request_ids[:, None] == request_grid[None, :], cache_len[None, :], 0), axis=1
    )
    positions = (starts + token_ids % span_len).astype(jnp.float32)
    rotated_q = rotate(queries.astype(jnp.float32), positions).astype(jnp.bfloat16)
    rotated_k = rotate(keys.astype(jnp.float32), positions).astype(jnp.bfloat16)
    core = device_at % 2
    half = head_count // 2
    chip_len = 2 * tok_dev

    def halves(x):
        return (
            lax.dynamic_slice_in_dim(x, core * half, half, 0),
            lax.dynamic_slice_in_dim(x, (1 - core) * half, half, 0),
        )

    def in_order(mine, got, axis):
        return jnp.where(
            core == 0,
            jnp.concatenate([mine, got], axis=axis),
            jnp.concatenate([got, mine], axis=axis),
        )

    q_own = jnp.transpose(rotated_q, (1, 0, 2))
    q_mine, q_other = halves(q_own)
    q_places = gather_lines(in_order(q_mine, swap(q_other, 1), 1))
    all_k = lax.all_gather(rotated_k, "pages", axis=0, tiled=True)
    all_v = lax.all_gather(values, "pages", axis=0, tiled=True)
    natural = Layout((0, 1, 2))
    all_k = with_layout_constraint(all_k, natural)
    all_v = with_layout_constraint(all_v, natural)
    weight = lax.all_gather(out_weight, "pages", axis=1, tiled=True)

    my_slots = device_at * slot_count + jnp.arange(slot_count, dtype=jnp.int32)
    chip_slots = jnp.concatenate(
        [my_slots, (device_at ^ 1) * slot_count + jnp.arange(slot_count, dtype=jnp.int32)]
    )
    cached_hit = page_table.reshape(-1)[None, :] == chip_slots[:, None]
    fresh_hit = append_slots.reshape(-1)[None, :] == my_slots[:, None]
    table_at = jnp.arange(requests * max_pages, dtype=jnp.int32)
    shown = (table_at % max_pages) * PAGE < jnp.repeat(cache_len, max_pages)
    is_fresh = jnp.any(fresh_hit, axis=1)
    fresh_index = jnp.sum(
        jnp.where(fresh_hit, jnp.arange(requests * new_pages, dtype=jnp.int32)[None, :], 0), axis=1
    )
    slot_key = requests - jnp.sum(
        jnp.where(cached_hit & shown[None, :], requests - (table_at // max_pages)[None, :], 0),
        axis=1,
    )
    slot_at = jnp.arange(2 * slot_count, dtype=jnp.int32)
    earlier = (slot_key[None, :] < slot_key[:, None]) | (
        (slot_key[None, :] == slot_key[:, None]) & (slot_at[None, :] < slot_at[:, None])
    )
    rank = jnp.sum(earlier.astype(jnp.int32), axis=1)
    order = jnp.sum(jnp.where(rank[None, :] == slot_at[:, None], slot_at[None, :], 0), axis=1)
    slot_starts = jnp.sum((slot_key[None, :] < request_grid[:, None]).astype(jnp.int32), axis=1)
    slot_counts = jnp.sum((slot_key[None, :] == request_grid[:, None]).astype(jnp.int32), axis=1)

    k_mine, k_other = halves(jnp.transpose(key_cache, (2, 0, 1, 3)))
    v_mine, v_other = halves(jnp.transpose(value_cache, (2, 0, 3, 1)))
    k_heads = jnp.concatenate([k_mine, swap(k_other, 1)], axis=1)
    v_heads = jnp.concatenate([v_mine, swap(v_other, 1)], axis=1)

    line = page_devs // 4
    line_at, across = device_at // 4, (device_at // 2) % 2
    outs = cached_attention(
        [q for q, _, _, _ in q_places],
        [jnp.clip(at, 0, line - 1) * 2 + side for _, at, side, _ in q_places],
        [ok for _, _, _, ok in q_places],
        [((line_at + k) % line) * 2 + (across ^ d) for k in range(line) for d in range(2)],
        k_heads,
        v_heads,
        order,
        slot_starts,
        slot_counts,
        span_len,
        scale2,
    )
    unit = math.gcd(span_len, chip_len)
    merged = lambda parts, ok: merge(parts, ok, chip_len, unit, scale2)
    chip_part = merge_lines([outs[2 * k : 2 * k + 2] for k in range(line)], merged)
    other_part = swap(chip_part, 1)
    per_unit, units, _ = stat_rows_of(chip_len, unit)

    def own_tokens(part):
        rows = lax.dynamic_slice_in_dim(part[:, :chip_len], core * tok_dev, tok_dev, 1)
        stats = part[:, chip_len : chip_len + 3 * units * per_unit].astype(jnp.float32)
        stats = stats.reshape(half, 3, units, per_unit * 128)[..., :unit]
        stats = stats.reshape(half, 3, chip_len)
        stats = lax.dynamic_slice_in_dim(stats, core * tok_dev, tok_dev, 2)
        return rows.astype(jnp.float32), stats[:, 0], stats[:, 1] + stats[:, 2]

    cached_mean, cached_top, cached_total = [
        in_order(mine, got, 0)
        for mine, got in zip(own_tokens(chip_part), own_tokens(other_part))
    ]

    window_at = jnp.minimum(request_ids[0], requests - 2) * span_len
    k_window = lax.dynamic_slice_in_dim(all_k, window_at, 2 * span_len, 0)
    v_window = lax.dynamic_slice_in_dim(all_v, window_at, 2 * span_len, 0)
    token_rows = jnp.stack([token_ids, request_ids * span_len])
    key_cols = (window_at + jnp.arange(2 * span_len, dtype=jnp.int32))[:, None]
    fresh_sum, fresh_top, fresh_total = fresh_attention(
        q_own,
        jnp.transpose(k_window, (1, 0, 2)),
        jnp.transpose(v_window, (1, 2, 0)),
        token_rows,
        key_cols,
        scale2,
    )
    fresh_sum = jnp.transpose(fresh_sum, (0, 2, 1))
    fresh_top = fresh_top[:, 0]
    fresh_total = fresh_total[:, 0]
    best = jnp.maximum(cached_top, fresh_top)
    cached_part = cached_total * jnp.exp2((cached_top - best) * scale2)
    fresh_part = jnp.exp2((fresh_top - best) * scale2)
    total = cached_part + fresh_total * fresh_part
    attended = (
        cached_mean * (cached_part / total)[..., None] + fresh_sum * (fresh_part / total)[..., None]
    ).astype(jnp.bfloat16)
    attended = jnp.transpose(attended, (1, 0, 2)).reshape(tok_dev, head_count * head_dim)

    projected = jnp.dot(attended, weight, preferred_element_type=jnp.float32)
    summed = lax.psum_scatter(
        projected.astype(jnp.bfloat16), "heads", scatter_dimension=1, tiled=True
    ).astype(jnp.float32)
    hidden = (summed + out_bias[None, :]).astype(jnp.bfloat16)

    page_shape = (requests * new_pages, PAGE, head_count, head_dim)
    key_out, value_out = write_pages(
        key_cache,
        value_cache,
        all_k.reshape(page_shape),
        all_v.reshape(page_shape),
        is_fresh,
        fresh_index,
    )
    return (hidden, key_out, value_out)


def solution(mesh):
    placed = (
        P("pages", "heads", None),
        P("pages", "heads", None),
        P("pages", "heads", None),
        P("pages", None, "heads", None),
        P("pages", None, "heads", None),
        P(),
        P(),
        P(),
        P("heads", "pages"),
        P("heads"),
    )
    return jax.shard_map(
        per_device,
        mesh=mesh,
        in_specs=placed,
        out_specs=(
            P("pages", "heads"),
            P("pages", None, "heads", None),
            P("pages", None, "heads", None),
        ),
        check_vma=False,
    )
```

profile of v0, /device:TPU:12, one launch (start us, length us, event | category | flops | bytes accessed | tf_op | source)
XLA Modules:
  0.0 432.2 jit_solution(6230720519209789073)
XLA Ops:
  30.1 7.2 %constant_dynamic-slice_fusion.5 = (bf16[12,128,4,128]{3,2,1,0:T(4,128)(2,1)}, bf16[12,128,4,128]{3,2,1,0:T(4,128)(2,1)}, bf16[12,128,4,128]{3,2,1,0:T(4,128)(2,1)S(1)}, bf16[12,128,4,128]{3,2,1,0:T(4,128)(2,1)}) fusion(bf16[12,128,8,128]{3,2,1,0:T(8,128)(2,1)S(1)} %copy-done, s32[]{:T(128)S(6)} %select_n.189, s32[]{:T(128)S(6)} %select_n.190, ...), kind=kLoop, calls=%fused_computation.67 | loop fusion | bytes 12582920 | tf_op jit(solution)/shard_map/dynamic-slice.4
  43.6 12.4 %collective-permute-done.2.refs_7_ = bf16[4,576,128]{2,1,0:T(8,128)(2,1)} collective-permute-done((bf16[4,576,128]{2,1,0:T(8,128)(2,1)}, bf16[4,576,128]{2,1,0:T(8,128)(2,1)}, u32[]{:S(2)}, u32[]{:S(2)}) %collective-permute-start.2) | collective-permute-done | bytes 589856 | tf_op jit(solution)/shard_map/ppermute | solution.py:270
  56.0 5.2 %collective-permute-start.6 = (bf16[4,576,128]{2,1,0:T(8,128)(2,1)}, bf16[4,576,128]{2,1,0:T(8,128)(2,1)}, u32[]{:S(2)}, u32[]{:S(2)}) collective-permute-start(bf16[4,576,128]{2,1,0:T(8,128)(2,1)} %collective-permute-done.2.refs_7_), channel_id=1, source_target_pairs={{4,8},{5,9},{6,10},{7,11},{8,12},{9,13},{10,14},{11,15},{20,24},{2... | collective-permute-start | bytes 1769480 | tf_op jit(solution)/shard_map/ppermute | solution.py:270
  65.5 35.3 %collective-permute-done.6.refs_11_ = bf16[4,576,128]{2,1,0:T(8,128)(2,1)} collective-permute-done((bf16[4,576,128]{2,1,0:T(8,128)(2,1)}, bf16[4,576,128]{2,1,0:T(8,128)(2,1)}, u32[]{:S(2)}, u32[]{:S(2)}) %collective-permute-start.6) | collective-permute-done | bytes 589856 | tf_op jit(solution)/shard_map/ppermute | solution.py:270
  120.2 8.5 %collective-permute-done.12.refs_17_ = bf16[4,576,128]{2,1,0:T(8,128)(2,1)} collective-permute-done((bf16[4,576,128]{2,1,0:T(8,128)(2,1)}, bf16[4,576,128]{2,1,0:T(8,128)(2,1)}, u32[]{:S(2)}, u32[]{:S(2)}) %collective-permute-start.12) | collective-permute-done | bytes 589856 | tf_op jit(solution)/shard_map/ppermute | solution.py:270
  137.0 9.5 %collective-permute-done.9.refs_14_ = bf16[4,576,128]{2,1,0:T(8,128)(2,1)S(1)} collective-permute-done((bf16[4,576,128]{2,1,0:T(8,128)(2,1)}, bf16[4,576,128]{2,1,0:T(8,128)(2,1)S(1)}, u32[]{:S(2)}, u32[]{:S(2)}) %collective-permute-start.9) | collective-permute-done | bytes 589856 | tf_op jit(solution)/shard_map/ppermute | solution.py:292
  146.5 36.9 %cached_attention.1 = (bf16[4,608,128]{2,1,0:T(8,128)(2,1)S(1)}, bf16[4,608,128]{2,1,0:T(8,128)(2,1)S(1)}, bf16[4,608,128]{2,1,0:T(8,128)(2,1)S(1)}, bf16[4,608,...) custom-call(s32[22]{0:T(128)S(1)} %stack.185.refs_0_, ...), custom_call_target="tpu_custom_call" | custom-call | tf_op jit(solution)/shard_map/cached_attention/pallas_call | solution.py:154
  189.7 19.5 %collective-permute-done.17.refs_2_ = bf16[4,608,128]{2,1,0:T(8,128)(2,1)S(1)} collective-permute-done((bf16[4,608,128]{2,1,0:T(8,128)(2,1)S(1)}, bf16[4,608,128]{2,1,0:T(8,128)(2,1)S(1)}, u32[]{:S(2)}, u32[]{:S(2)}) %collective-permute-start.17) | collective-permute-done | bytes 622624 | tf_op jit(solution)/shard_map/ppermute | solution.py:264
  216.0 6.5 %collective-permute-done.19.refs_2_ = bf16[4,608,128]{2,1,0:T(8,128)(2,1)} collective-permute-done((bf16[4,608,128]{2,1,0:T(8,128)(2,1)}, bf16[4,608,128]{2,1,0:T(8,128)(2,1)}, u32[]{:S(2)}, u32[]{:S(2)}) %collective-permute-start.19) | collective-permute-done | bytes 622624 | tf_op jit(solution)/shard_map/ppermute | solution.py:264
  222.6 4.6 %merge.12.refs_1_ = bf16[4,608,128]{2,1,0:T(8,128)(2,1)} custom-call(s32[2]{0:T(128)} %copy-done.20, bf16[4,608,128]{2,1,0:T(8,128)(2,1)} %copy-done.8, bf16[4,608,128]{2,1,0:T(8,128)(2,1)} %collective-permute-done.19.refs_2_), custom_call_target="tpu_custom_call" | custom-call | tf_op jit(solution)/shard_map/merge/pallas_call | solution.py:217
  229.9 7.1 %collective-permute-done.18.refs_2_ = bf16[4,608,128]{2,1,0:T(8,128)(2,1)} collective-permute-done((bf16[4,608,128]{2,1,0:T(8,128)(2,1)}, bf16[4,608,128]{2,1,0:T(8,128)(2,1)}, u32[]{:S(2)}, u32[]{:S(2)}) %collective-permute-start.18) | collective-permute-done | bytes 622624 | tf_op jit(solution)/shard_map/ppermute | solution.py:264
  237.0 4.6 %merge.11.refs_1_ = bf16[4,608,128]{2,1,0:T(8,128)(2,1)} custom-call(s32[2]{0:T(128)} %copy-done.20, bf16[4,608,128]{2,1,0:T(8,128)(2,1)} %copy-done.7, bf16[4,608,128]{2,1,0:T(8,128)(2,1)} %collective-permute-done.18.refs_2_), custom_call_target="tpu_custom_call" | custom-call | tf_op jit(solution)/shard_map/merge/pallas_call | solution.py:217
  247.5 15.1 %collective-permute-done.20.refs_2_ = bf16[4,608,128]{2,1,0:T(8,128)(2,1)} collective-permute-done((bf16[4,608,128]{2,1,0:T(8,128)(2,1)}, bf16[4,608,128]{2,1,0:T(8,128)(2,1)}, u32[]{:S(2)}, u32[]{:S(2)}) %collective-permute-start.20) | collective-permute-done | bytes 622624 | tf_op jit(solution)/shard_map/ppermute | solution.py:270
  271.5 4.6 %merge.16 = bf16[4,608,128]{2,1,0:T(8,128)(2,1)} custom-call(s32[2]{0:T(128)} %fusion.23.refs_0_, bf16[4,608,128]{2,1,0:T(8,128)(2,1)} %merge.12.refs_1_, bf16[4,608,128]{2,1,0:T(8,128)(2,1)} %collective-permute-done.24.refs_2_), custom_call_target="tpu_custom_call" | custom-call | tf_op jit(solution)/shard_map/merge/pallas_call | solution.py:217
  276.1 4.7 %collective-permute-start.25 = (bf16[4,608,128]{2,1,0:T(8,128)(2,1)}, bf16[4,608,128]{2,1,0:T(8,128)(2,1)}, u32[]{:S(2)}, u32[]{:S(2)}) collective-permute-start(bf16[4,608,128]{2,1,0:T(8,128)(2,1)} %merge.16), channel_id=1, source_target_pairs={{4,0},{5,1},{6,2},{7,3},{8,4},{9,5},{10,6},{11,7},{12,8},{13,9},{1... | collective-permute-start | bytes 1867784 | tf_op jit(solution)/shard_map/ppermute | solution.py:270
  280.8 15.6 %collective-permute-done.21.refs_2_ = bf16[4,608,128]{2,1,0:T(8,128)(2,1)} collective-permute-done((bf16[4,608,128]{2,1,0:T(8,128)(2,1)}, bf16[4,608,128]{2,1,0:T(8,128)(2,1)}, u32[]{:S(2)}, u32[]{:S(2)}) %collective-permute-start.21) | collective-permute-done | bytes 622624 | tf_op jit(solution)/shard_map/ppermute | solution.py:270
  305.8 4.6 %merge.9.refs_1_ = bf16[4,608,128]{2,1,0:T(8,128)(2,1)} custom-call(s32[2]{0:T(128)} %copy-done.20, bf16[4,608,128]{2,1,0:T(8,128)(2,1)} %copy-done.6, bf16[4,608,128]{2,1,0:T(8,128)(2,1)} %collective-permute-done.16.refs_2_), custom_call_target="tpu_custom_call" | custom-call | tf_op jit(solution)/shard_map/merge/pallas_call | solution.py:217
  310.5 15.9 %collective-permute-done.22.refs_2_ = bf16[4,608,128]{2,1,0:T(8,128)(2,1)} collective-permute-done((bf16[4,608,128]{2,1,0:T(8,128)(2,1)}, bf16[4,608,128]{2,1,0:T(8,128)(2,1)}, u32[]{:S(2)}, u32[]{:S(2)}) %collective-permute-start.22) | collective-permute-done | bytes 622624 | tf_op jit(solution)/shard_map/ppermute | solution.py:270
  326.3 5.0 %merge.17 = bf16[4,608,128]{2,1,0:T(8,128)(2,1)} custom-call(s32[3]{0:T(128)} %pad_add_fusion.4.refs_0_, bf16[4,608,128]{2,1,0:T(8,128)(2,1)} %merge.9.refs_1_, bf16[4,608,128]{2,1,0:T(8,128)(2,1)} %collective-permute-done.22.refs_2_, bf16[4,608,128]{2,1,0:T(8,128)(2,1)} %collective-permute-done.25.refs_3_), custom_call_target="tpu_custom_call" | custom-call | tf_op jit(solution)/shard_map/merge/pallas_call | solution.py:217
  354.7 5.0 %copy.105 = bf16[1536,8,128]{0,2,1:T(8,128)(2,1)} copy(bf16[1536,8,128]{2,1,0:T(8,128)(2,1)} %constant_dynamic-slice_fusion) | data formatting | bytes 6291456
  365.7 13.7 %fresh_attention.1 = (f32[8,128,288]{2,1,0:T(8,128)S(1)}, f32[8,1,288]{2,1,0:T(1,128)S(1)}, f32[8,1,288]{2,1,0:T(1,128)S(1)}) custom-call(bf16[8,288,128]{2,1,0:T(8,128)(2,1)S(1)} %copy-done.5, bf16[8,1536,128]{2,1,0:T(8,128)(2,1)S(1)} %bitcast.90, bf16[8,128,1536]{2,1,0:T(8,128)(2,1)S(1)} %bitcast.91, s32[2,288]{1,0:T(2,128)S(1)} %pad_add_fusion.refs_3_, ...), custom_call_target="tpu_custom_call" | custom-call | tf_op jit(solution)/shard_map/fresh_attention/pallas_call | solution.py:346
  380.7 7.9 %convolution_convert_fusion = bf16[288,4096]{1,0:T(8,128)(2,1)} fusion(bf16[288,1024]{0,1:T(8,128)(2,1)} %bitcast.97, bf16[1024,4096]{1,0:T(8,128)(2,1)} %all-gather.8.cloned.1.call-done), kind=kOutput, calls=%fused_computation | convolution fusion | flops 2417098752 | bytes 11337728 | tf_op jit(solution)/shard_map/dot_general | solution.py:518
  391.6 9.1 %write_pages.1 = (bf16[12,128,8,128]{3,2,1,0:T(8,128)(2,1)}, bf16[12,128,8,128]{3,2,1,0:T(8,128)(2,1)}) custom-call(s32[12]{0:T(128)S(1)} %convert_element_type.71.fresh_ref, s32[12]{0:T(128)S(1)} %fusion.13.index_ref, bf16[12,128,8,128]{3,2,1,0:T(8,128)(2,1)S(1)} %copy-done.1, bf16[12,128,8,128]{3,2,1,0:T(8,128)(2,1)S(1)} %copy-done, ...), custom_call_target="tpu_custom_call" | custom-call | tf_op jit(solution)/shard_map/write_pages/pallas_call | solution.py:248
  400.7 22.4 %reduce-scatter.2.cloned.1.call-done = bf16[288,2048]{1,0:T(8,128)(2,1)} async-done(((bf16[288,4096]{1,0:T(8,128)(2,1)}), bf16[288,2048]{1,0:T(8,128)(2,1)}) %reduce-scatter.2.cloned.1.call-update) | async-done | bytes 1179664 | tf_op jit(solution)/shard_map/reduce_scatter | solution.py:519
  (187 shorter events, 136.2 us)
Async XLA Ops:
  7.2 340.2 %all-gather.4.cloned.1.call-start = ((), (), s32[]{:S(2)}) async-start(), calls=%async_computation.1 | async-start | bytes 10027008 | tf_op jit(solution)/shard_map/all_gather | solution.py:422
  13.8 337.7 %all-gather.6.cloned.1.call-start = ((), (), s32[]{:S(2)}) async-start(), calls=%async_computation.2 | async-start | bytes 10027008 | tf_op jit(solution)/shard_map/all_gather | solution.py:423
  14.6 366.1 %all-gather.8.cloned.1.call-start = ((), (), s32[]{:S(2)}) async-start(), calls=%async_computation.3 | async-start | bytes 8912896 | tf_op jit(solution)/shard_map/all_gather | solution.py:427
  15.3 407.8 %reduce-scatter.2.cloned.1.call-start = ((), (), s32[]{:S(2)}) async-start(), calls=%async_computation.4 | async-start | bytes 3538944 | tf_op jit(solution)/shard_map/reduce_scatter | solution.py:519
  23.4 32.6 %collective-permute-start.2 = (bf16[4,576,128]{2,1,0:T(8,128)(2,1)}, bf16[4,576,128]{2,1,0:T(8,128)(2,1)}, u32[]{:S(2)}, u32[]{:S(2)}) collective-permute-start(bf16[4,576,128]{2,1,0:T(8,128)(2,1)} %maximum_select_fusion.1.refs_5_), channel_id=1, source_target_pairs={{0,4},{1,5},{2,6},{3,7},{4,8},{5,9},{6,10},{7,11},{8,12},{9,13},{1... | collective-permute-start | bytes 1769480 | tf_op jit(solution)/shard_map/ppermute | solution.py:270
  26.9 34.3 %collective-permute-start.4 = (bf16[4,576,128]{2,1,0:T(8,128)(2,1)}, bf16[4,576,128]{2,1,0:T(8,128)(2,1)}, u32[]{:S(2)}, u32[]{:S(2)}) collective-permute-start(bf16[4,576,128]{2,1,0:T(8,128)(2,1)} %maximum_select_fusion.1.refs_5_), channel_id=1, source_target_pairs={{4,0},{5,1},{6,2},{7,3},{8,4},{9,5},{10,6},{11,7},{12,8},{13,9},{1... | collective-permute-start | bytes 1769480 | tf_op jit(solution)/shard_map/ppermute | solution.py:270
  38.8 76.0 %collective-permute-start.14 = (bf16[4,12,128,128]{3,2,1,0:T(8,128)(2,1)}, bf16[4,12,128,128]{3,2,1,0:T(8,128)(2,1)}, u32[]{:S(2)}, u32[]{:S(2)}) collective-permute-start(bf16[4,12,128,128]{3,2,1,0:T(8,128)(2,1)} %bitcast.86), channel_id=1, source_target_pairs={{0,1},{1,0},{2,3},{3,2},{4,5},{5,4},{6,7},{7,6},{8,9},{9,8},{10,11... | collective-permute-start | bytes 4718600 | tf_op jit(solution)/shard_map/ppermute | solution.py:264
  42.6 73.0 %collective-permute-start.15 = (bf16[4,12,128,128]{3,2,1,0:T(8,128)(2,1)}, bf16[4,12,128,128]{3,2,1,0:T(8,128)(2,1)}, u32[]{:S(2)}, u32[]{:S(2)}) collective-permute-start(bf16[4,12,128,128]{3,2,1,0:T(8,128)(2,1)} %bitcast.96), channel_id=1, source_target_pairs={{0,1},{1,0},{2,3},{3,2},{4,5},{5,4},{6,7},{7,6},{8,9},{9,8},{10,11... | collective-permute-start | bytes 4718600 | tf_op jit(solution)/shard_map/ppermute | solution.py:264
  56.0 44.8 %collective-permute-start.6 = (bf16[4,576,128]{2,1,0:T(8,128)(2,1)}, bf16[4,576,128]{2,1,0:T(8,128)(2,1)}, u32[]{:S(2)}, u32[]{:S(2)}) collective-permute-start(bf16[4,576,128]{2,1,0:T(8,128)(2,1)} %collective-permute-done.2.refs_7_), channel_id=1, source_target_pairs={{4,8},{5,9},{6,10},{7,11},{8,12},{9,13},{10,14},{11,15},{20,24},{2... | collective-permute-start | bytes 1769480 | tf_op jit(solution)/shard_map/ppermute | solution.py:270
  61.2 42.1 %collective-permute-start.8 = (bf16[4,576,128]{2,1,0:T(8,128)(2,1)}, bf16[4,576,128]{2,1,0:T(8,128)(2,1)}, u32[]{:S(2)}, u32[]{:S(2)}) collective-permute-start(bf16[4,576,128]{2,1,0:T(8,128)(2,1)} %collective-permute-done.4.refs_9_), channel_id=1, source_target_pairs={{4,0},{5,1},{6,2},{7,3},{8,4},{9,5},{10,6},{11,7},{20,16},{21,17},... | collective-permute-start | bytes 1769480 | tf_op jit(solution)/shard_map/ppermute | solution.py:270
  63.3 49.6 %collective-permute-start.3 = (bf16[4,576,128]{2,1,0:T(8,128)(2,1)}, bf16[4,576,128]{2,1,0:T(8,128)(2,1)}, u32[]{:S(2)}, u32[]{:S(2)}) collective-permute-start(bf16[4,576,128]{2,1,0:T(8,128)(2,1)} %collective-permute-done.2.refs_7_), channel_id=1, source_target_pairs={{4,6},{5,7},{6,4},{7,5},{8,10},{9,11},{10,8},{11,9},{12,14},{13,15... | collective-permute-start | bytes 1769480 | tf_op jit(solution)/shard_map/ppermute | solution.py:290
  103.3 25.4 %collective-permute-start.12 = (bf16[4,576,128]{2,1,0:T(8,128)(2,1)}, bf16[4,576,128]{2,1,0:T(8,128)(2,1)}, u32[]{:S(2)}, u32[]{:S(2)}) collective-permute-start(bf16[4,576,128]{2,1,0:T(8,128)(2,1)} %collective-permute-done.8.refs_13_), channel_id=1, source_target_pairs={{4,0},{5,1},{6,2},{7,3},{20,16},{21,17},{22,18},{23,19}} | collective-permute-start | bytes 1769480 | tf_op jit(solution)/shard_map/ppermute | solution.py:270
  112.9 24.1 %collective-permute-start.5 = (bf16[4,576,128]{2,1,0:T(8,128)(2,1)}, bf16[4,576,128]{2,1,0:T(8,128)(2,1)S(1)}, u32[]{:S(2)}, u32[]{:S(2)}) collective-permute-start(bf16[4,576,128]{2,1,0:T(8,128)(2,1)} %collective-permute-done.4.refs_9_), channel_id=1, source_target_pairs={{0,2},{1,3},{2,0},{3,1},{4,6},{5,7},{6,4},{7,5},{8,10},{9,11},{10,... | collective-permute-start | bytes 1769480 | tf_op jit(solution)/shard_map/ppermute | solution.py:292
  115.6 31.0 %collective-permute-start.9 = (bf16[4,576,128]{2,1,0:T(8,128)(2,1)}, bf16[4,576,128]{2,1,0:T(8,128)(2,1)S(1)}, u32[]{:S(2)}, u32[]{:S(2)}) collective-permute-start(bf16[4,576,128]{2,1,0:T(8,128)(2,1)} %collective-permute-done.8.refs_13_), channel_id=1, source_target_pairs={{0,2},{1,3},{2,0},{3,1},{4,6},{5,7},{6,4},{7,5},{16,18},{17,19},{1... | collective-permute-start | bytes 1769480 | tf_op jit(solution)/shard_map/ppermute | solution.py:292
  119.5 27.0 %collective-permute-start.11 = (bf16[4,576,128]{2,1,0:T(8,128)(2,1)}, bf16[4,576,128]{2,1,0:T(8,128)(2,1)S(1)}, u32[]{:S(2)}, u32[]{:S(2)}) collective-permute-start(bf16[4,576,128]{2,1,0:T(8,128)(2,1)} %collective-permute-done.10.refs_15_), channel_id=1, source_target_pairs={{12,14},{13,15},{14,12},{15,13},{28,30},{29,31},{30,28},{31,29}} | collective-permute-start | bytes 1769480 | tf_op jit(solution)/shard_map/ppermute | solution.py:290
  187.6 35.0 %collective-permute-start.19 = (bf16[4,608,128]{2,1,0:T(8,128)(2,1)}, bf16[4,608,128]{2,1,0:T(8,128)(2,1)}, u32[]{:S(2)}, u32[]{:S(2)}) collective-permute-start(bf16[4,608,128]{2,1,0:T(8,128)(2,1)} %get-tuple-element.23), channel_id=1, source_target_pairs={{0,2},{1,3},{2,0},{3,1},{4,6},{5,7},{6,4},{7,5},{8,10},{9,11},{10,... | collective-permute-start | bytes 1867784 | tf_op jit(solution)/shard_map/ppermute | solution.py:264
  189.6 47.4 %collective-permute-start.18 = (bf16[4,608,128]{2,1,0:T(8,128)(2,1)}, bf16[4,608,128]{2,1,0:T(8,128)(2,1)}, u32[]{:S(2)}, u32[]{:S(2)}) collective-permute-start(bf16[4,608,128]{2,1,0:T(8,128)(2,1)} %get-tuple-element.21), channel_id=1, source_target_pairs={{0,2},{1,3},{2,0},{3,1},{4,6},{5,7},{6,4},{7,5},{8,10},{9,11},{10,... | collective-permute-start | bytes 1867784 | tf_op jit(solution)/shard_map/ppermute | solution.py:264
  214.6 27.0 %collective-permute-start.23 = (bf16[4,608,128]{2,1,0:T(8,128)(2,1)}, bf16[4,608,128]{2,1,0:T(8,128)(2,1)}, u32[]{:S(2)}, u32[]{:S(2)}) collective-permute-start(bf16[4,608,128]{2,1,0:T(8,128)(2,1)} %merge.10.refs_1_), channel_id=1, source_target_pairs={{12,8},{13,9},{14,10},{15,11},{28,24},{29,25},{30,26},{31,27}} | collective-permute-start | bytes 1867784 | tf_op jit(solution)/shard_map/ppermute | solution.py:270
  227.2 35.4 %collective-permute-start.20 = (bf16[4,608,128]{2,1,0:T(8,128)(2,1)}, bf16[4,608,128]{2,1,0:T(8,128)(2,1)}, u32[]{:S(2)}, u32[]{:S(2)}) collective-permute-start(bf16[4,608,128]{2,1,0:T(8,128)(2,1)} %merge.12.refs_1_), channel_id=1, source_target_pairs={{0,4},{1,5},{2,6},{3,7},{16,20},{17,21},{18,22},{19,23}} | collective-permute-start | bytes 1867784 | tf_op jit(solution)/shard_map/ppermute | solution.py:270
  246.2 25.2 %collective-permute-start.24 = (bf16[4,608,128]{2,1,0:T(8,128)(2,1)}, bf16[4,608,128]{2,1,0:T(8,128)(2,1)}, u32[]{:S(2)}, u32[]{:S(2)}) collective-permute-start(bf16[4,608,128]{2,1,0:T(8,128)(2,1)} %merge.15), channel_id=1, source_target_pairs={{8,4},{9,5},{10,6},{11,7},{12,8},{13,9},{14,10},{15,11},{24,20},{2... | collective-permute-start | bytes 1867784 | tf_op jit(solution)/shard_map/ppermute | solution.py:270
  267.2 29.2 %collective-permute-start.21 = (bf16[4,608,128]{2,1,0:T(8,128)(2,1)}, bf16[4,608,128]{2,1,0:T(8,128)(2,1)}, u32[]{:S(2)}, u32[]{:S(2)}) collective-permute-start(bf16[4,608,128]{2,1,0:T(8,128)(2,1)} %merge.13), channel_id=1, source_target_pairs={{0,4},{1,5},{2,6},{3,7},{4,8},{5,9},{6,10},{7,11},{16,20},{17,21},... | collective-permute-start | bytes 1867784 | tf_op jit(solution)/shard_map/ppermute | solution.py:270
  269.7 36.1 %collective-permute-start.16 = (bf16[4,608,128]{2,1,0:T(8,128)(2,1)}, bf16[4,608,128]{2,1,0:T(8,128)(2,1)}, u32[]{:S(2)}, u32[]{:S(2)}) collective-permute-start(bf16[4,608,128]{2,1,0:T(8,128)(2,1)} %copy-done.10), channel_id=1, source_target_pairs={{0,2},{1,3},{2,0},{3,1},{4,6},{5,7},{6,4},{7,5},{8,10},{9,11},{10,... | collective-permute-start | bytes 1867784 | tf_op jit(solution)/shard_map/ppermute | solution.py:264
  276.1 34.4 %collective-permute-start.25 = (bf16[4,608,128]{2,1,0:T(8,128)(2,1)}, bf16[4,608,128]{2,1,0:T(8,128)(2,1)}, u32[]{:S(2)}, u32[]{:S(2)}) collective-permute-start(bf16[4,608,128]{2,1,0:T(8,128)(2,1)} %merge.16), channel_id=1, source_target_pairs={{4,0},{5,1},{6,2},{7,3},{8,4},{9,5},{10,6},{11,7},{12,8},{13,9},{1... | collective-permute-start | bytes 1867784 | tf_op jit(solution)/shard_map/ppermute | solution.py:270
  301.0 25.3 %collective-permute-start.22 = (bf16[4,608,128]{2,1,0:T(8,128)(2,1)}, bf16[4,608,128]{2,1,0:T(8,128)(2,1)}, u32[]{:S(2)}, u32[]{:S(2)}) collective-permute-start(bf16[4,608,128]{2,1,0:T(8,128)(2,1)} %merge.14), channel_id=1, source_target_pairs={{0,4},{1,5},{2,6},{3,7},{4,8},{5,9},{6,10},{7,11},{8,12},{9,13},{1... | collective-permute-start | bytes 1867784 | tf_op jit(solution)/shard_map/ppermute | solution.py:270
  (32 other events, 275.3 us)
Sparse Core Ops, SparseCore 0:
  14.0 108.1 all-gather.3
  124.5 91.3 all-gather.5
  218.1 110.4 all-gather.7
  388.7 34.3 reduce-scatter.1
where the time goes:
time: 434 us; the launch traced here: 432 us
  waiting for transfers between devices  172 us (40%)
  Pallas kernels  102 us (24%)
  local copies, waits for them, and re-layouts  59 us (14%)
  starting transfers between devices  45.3 us (10%)
  other arithmetic  31.2 us (7%)
  between operations  15 us (3%)
  matrix products  7.87 us (2%)
    ppermute x12, waiting for transfers between devices, shift(): return lax.ppermute(x, 'pages', moves)  104 us
    pallas_call x9, Pallas kernels, merge(): pl.pallas_call(lambda *refs: merge_kernel(unit, part_len, scale2, *refs),...  41.9 us
    pallas_call x1, Pallas kernels, cached_attention(): pl.pallas_call(lambda *refs: cached_kernel(unit, span, scale2, places, *r...  36.9 us
    unnamed x59, local copies, waits for them, and re-layouts  36 us
    ppermute x9, waiting for transfers between devices, swap(): return lax.ppermute(x, 'pages', [(p, p ^ bit) for p in range(devs)])  35.1 us
    ppermute x12, starting transfers between devices, shift(): return lax.ppermute(x, 'pages', moves)  30.1 us
    reduce_scatter x1, waiting for transfers between devices, per_device(): lax.psum_scatter(projected.astype(jnp.bfloat16), 'heads', scatter_dimensi...  22.4 us
    pallas_call x1, Pallas kernels, fresh_attention(): pl.pallas_call(lambda *refs: fresh_kernel(scale2, *refs), grid=(heads,),...  13.7 us
  transfers between devices with their start and end apart: 31, of which 13 were waited for; matrix products, arithmetic and copies ran while one was open for 16% of the time, Pallas kernels for 23%

commit v1 on v0

--- a/solution.py
+++ b/solution.py
@@ -5,7 +5,6 @@
 import jax.numpy as jnp
 from jax import lax
 from jax.experimental import pallas as pl
-from jax.experimental.layout import Layout, with_layout_constraint
 from jax.experimental.pallas import tpu as pltpu
 from jax.sharding import PartitionSpec as P
 
@@ -54,7 +53,7 @@
     return jnp.concatenate(rows, axis=0).astype(jnp.bfloat16)
 
 
-def cached_kernel(unit, span, scale2, places, at_ref, ok_ref, order_ref, start_ref, count_ref,
+def cached_kernel(unit, stat_unit, span, scale2, places, at_ref, ok_ref, order_ref, start_ref, count_ref,
                   *refs):
     q_refs, (k_ref, v_ref), refs = refs[:places], refs[places : places + 2], refs[places + 2 :]
     o_refs, (q_all, o_all, s_all, q_scr, m_scr, l_scr, acc_scr) = refs[:-7], refs[-7:]
@@ -62,7 +61,7 @@
     chips, part_len, _ = q_all.shape
     per_part = part_len // unit
     per_request = span // unit
-    per_unit, _, pad_to = stat_rows_of(part_len, unit)
+    per_unit, units, pad_to = stat_rows_of(part_len, stat_unit)
 
     for index in range(places):
 
@@ -70,13 +69,12 @@
         def _(index=index):
             q_all[at_ref[index]] = q_refs[index][0]
 
-    def place(request, index):
-        at = request * per_request + index
+    def place(at, per_part):
         return at // per_part, at % per_part
 
     def one_request(request, _):
         for index in range(per_request):
-            part, piece = place(request, index)
+            part, piece = place(request * per_request + index, per_part)
             row = pl.ds(pl.multiple_of(piece * unit, unit), unit)
             q_scr[index * unit : (index + 1) * unit, :] = q_all[part, row, :]
         first = start_ref[request]
@@ -123,13 +121,15 @@
         high = totals.astype(jnp.bfloat16).astype(jnp.float32)
         kinds = [sent, high, totals - high]
         for index in range(per_request):
-            part, piece = place(request, index)
-            cols = slice(index * unit, (index + 1) * unit)
+            part, piece = place(request * per_request + index, per_part)
             row = pl.ds(pl.multiple_of(piece * unit, unit), unit)
-            o_all[part, row, :] = out[cols, :]
+            o_all[part, row, :] = out[index * unit : (index + 1) * unit, :]
+        for index in range(span // stat_unit):
+            part, piece = place(request * (span // stat_unit) + index, units)
+            cols = slice(index * stat_unit, (index + 1) * stat_unit)
             for kind, values in enumerate(kinds):
                 for r, line in enumerate(stat_rows(values[:, cols])):
-                    at = (kind * per_part + piece) * per_unit + r
+                    at = (kind * units + piece) * per_unit + r
                     s_all[part, pl.ds(at, 1), :] = line
         return 0
 
@@ -141,18 +141,18 @@
 
 
 def cached_attention(q_places, at, ok, out_at, k_heads, v_heads, order, starts, counts, span,
-                     scale2):
+                     stat_unit, scale2):
     places = len(q_places)
     chips = len(out_at)
     heads, part_len, head_dim = q_places[0].shape
     slots = k_heads.shape[1]
     unit = math.gcd(span, part_len)
-    _, _, pad_to = stat_rows_of(part_len, unit)
+    _, _, pad_to = stat_rows_of(part_len, stat_unit)
     own_block = lambda *dims: pl.BlockSpec(
         (1,) + dims, lambda h, *_: (h,) + (0,) * len(dims)
     )
     return pl.pallas_call(
-        lambda *refs: cached_kernel(unit, span, scale2, places, *refs),
+        lambda *refs: cached_kernel(unit, stat_unit, span, scale2, places, *refs),
         grid_spec=pltpu.PrefetchScalarGridSpec(
             num_scalar_prefetch=5,
             grid=(heads,),
@@ -177,11 +177,17 @@
     )(jnp.stack(at + out_at), jnp.stack(ok), order, starts, counts, *q_places, k_heads, v_heads)
 
 
+def spread(row, width, unit):
+    return jnp.broadcast_to(row, (width, row.shape[1])).T[:unit]
+
+
 def merge_kernel(unit, part_len, scale2, ok_ref, *refs):
     in_refs, out_ref = refs[:-1], refs[-1]
     head_dim = out_ref.shape[2]
     per_unit, units, pad_to = stat_rows_of(part_len, unit)
     stats = [ref[0, part_len:, :].astype(jnp.float32) for ref in in_refs]
+    rows = [ref[0, :part_len, :].astype(jnp.float32) for ref in in_refs]
+    outs = []
     kinds = [[], [], []]
     for u in range(units):
 
@@ -199,16 +205,15 @@
         shares = [t * jnp.exp2((p - top) * scale2) for t, p in zip(totals, peaks)]
         total = functools.reduce(jnp.add, shares)
         inverse = 1.0 / jnp.maximum(total, 1e-30)
-        rows = slice(u * unit, (u + 1) * unit)
         merged = None
-        for ref, share in zip(in_refs, shares):
-            part = jnp.broadcast_to(share * inverse, (head_dim, share.shape[1])).T[:unit]
-            part = part * ref[0, rows, :].astype(jnp.float32)
+        for values, share in zip(rows, shares):
+            part = spread(share * inverse, head_dim, unit) * values[u * unit : (u + 1) * unit]
             merged = part if merged is None else merged + part
-        out_ref[0, rows, :] = merged.astype(jnp.bfloat16)
+        outs.append(merged)
         high = total.astype(jnp.bfloat16).astype(jnp.float32)
         for kind, value in zip(kinds, (top, high, total - high)):
             kind.append(value)
+    out_ref[0, :part_len, :] = jnp.concatenate(outs, axis=0).astype(jnp.bfloat16)
     out_ref[0, part_len:, :] = stat_block(kinds, pad_to)
 
 
@@ -268,6 +273,17 @@
     devs = lax.axis_size("pages")
     moves = [(p, p + 4 * hop) for p in range(devs) if p // 4 in senders]
     return lax.ppermute(x, "pages", moves)
+
+
+def gather_line(x):
+    line = lax.axis_size("pages") // 4
+    groups = [[g + 4 * i for i in range(line)] for g in range(4)]
+    return lax.all_gather(x, "pages", axis=0, tiled=False, axis_index_groups=groups)
+
+
+def spread_across(here):
+    across = swap(here, 2)
+    return [here, swap(here, 1), across, swap(across, 1)]
 
 
 def gather_lines(x):
@@ -320,7 +336,7 @@
     return merged([share(0), up, down], [yes, at >= 1, at <= line - 2])
 
 
-def fresh_kernel(scale2, q_ref, k_ref, v_ref, tok_ref, key_ref, o_ref, m_ref, l_ref):
+def fresh_kernel(unit, scale2, q_ref, k_ref, v_ref, tok_ref, key_ref, o_ref, s_ref):
     scores = lax.dot_general(
         k_ref[0], q_ref[0], (((1,), (1,)), ((), ())), preferred_element_type=jnp.float32
     )
@@ -331,20 +347,28 @@
     scores = jnp.where(visible, scores, low_score)
     peak = jnp.max(scores, axis=0, keepdims=True)
     weights = jnp.where(visible, jnp.exp2((scores - peak) * scale2), 0.0)
-    m_ref[0] = peak
-    l_ref[0] = jnp.sum(weights, axis=0, keepdims=True)
-    o_ref[0] = jnp.dot(
-        v_ref[0], weights.astype(jnp.bfloat16), preferred_element_type=jnp.float32
-    )
-
-
-def fresh_attention(q_own, k_window, v_window, token_rows, key_cols, scale2):
+    out = jnp.dot(v_ref[0], weights.astype(jnp.bfloat16), preferred_element_type=jnp.float32)
+    tok_dev = out.shape[1]
+    pad = -tok_dev % 128
+    out = jnp.concatenate([out, jnp.zeros((out.shape[0], pad), jnp.float32)], axis=1)
+    o_ref[0] = out.T[:tok_dev]
+    totals = jnp.sum(weights, axis=0, keepdims=True)
+    lines = []
+    for values in (peak, totals):
+        for at in range(0, tok_dev, unit):
+            lines += stat_rows(values[:, at : at + unit])
+    lines.append(jnp.zeros((s_ref.shape[1] - len(lines), 128), jnp.float32))
+    s_ref[0] = jnp.concatenate(lines, axis=0)
+
+
+def fresh_attention(q_own, k_window, v_window, token_rows, key_cols, unit, scale2):
     heads, tok_dev, head_dim = q_own.shape
     window = k_window.shape[1]
+    lines = -(-2 * (tok_dev // unit) * -(-unit // 128) // 8) * 8
     own = lambda h: (h, 0, 0)
     fixed = lambda h: (0, 0)
     return pl.pallas_call(
-        lambda *refs: fresh_kernel(scale2, *refs),
+        lambda *refs: fresh_kernel(unit, scale2, *refs),
         grid=(heads,),
         in_specs=[
             pl.BlockSpec((1, tok_dev, head_dim), own),
@@ -354,18 +378,159 @@
             pl.BlockSpec(key_cols.shape, fixed),
         ],
         out_specs=[
-            pl.BlockSpec((1, head_dim, tok_dev), own),
-            pl.BlockSpec((1, 1, tok_dev), own),
-            pl.BlockSpec((1, 1, tok_dev), own),
+            pl.BlockSpec((1, tok_dev, head_dim), own),
+            pl.BlockSpec((1, lines, 128), own),
         ],
         out_shape=[
-            jax.ShapeDtypeStruct((heads, head_dim, tok_dev), jnp.float32),
-            jax.ShapeDtypeStruct((heads, 1, tok_dev), jnp.float32),
-            jax.ShapeDtypeStruct((heads, 1, tok_dev), jnp.float32),
+            jax.ShapeDtypeStruct((heads, tok_dev, head_dim), jnp.float32),
+            jax.ShapeDtypeStruct((heads, lines, 128), jnp.float32),
         ],
         compiler_params=pltpu.CompilerParams(vmem_limit_bytes=40 * 2**20),
         name="fresh_attention",
     )(q_own, k_window, v_window, token_rows, key_cols)
+
+
+def finish_kernel(unit, half, scale2, core_ref, mine_ref, other_ref, fo_ref, fs_ref, out_ref):
+    core = core_ref[0]
+    tok_dev, head_dim = out_ref.shape
+    per_unit, units, _ = stat_rows_of(2 * tok_dev, unit)
+    here = pl.program_id(0) // half == core
+    part = jnp.where(
+        here, mine_ref[0].astype(jnp.float32), other_ref[0].astype(jnp.float32)
+    )
+    rows = jnp.where(core == 0, part[:tok_dev], part[tok_dev : 2 * tok_dev])
+    stats = part[2 * tok_dev :]
+    fresh_stats = fs_ref[0]
+
+    def line(block, at):
+        pieces = [block[at + r : at + r + 1, :] for r in range(per_unit)]
+        return jnp.concatenate(pieces, axis=1)
+
+    def cached_line(kind, u):
+        first = line(stats, (kind * units + u) * per_unit)
+        return jnp.where(core == 0, first, line(stats, (kind * units + units // 2 + u) * per_unit))
+
+    outs = []
+    for u in range(units // 2):
+        cached_top = cached_line(0, u)
+        cached_total = cached_line(1, u) + cached_line(2, u)
+        fresh_top = line(fresh_stats, u * per_unit)
+        fresh_total = line(fresh_stats, (units // 2 + u) * per_unit)
+        best = jnp.maximum(cached_top, fresh_top)
+        cached_share = cached_total * jnp.exp2((cached_top - best) * scale2)
+        fresh_share = jnp.exp2((fresh_top - best) * scale2)
+        inverse = 1.0 / jnp.maximum(cached_share + fresh_total * fresh_share, 1e-30)
+        at = slice(u * unit, (u + 1) * unit)
+        outs.append(
+            rows[at] * spread(cached_share * inverse, head_dim, unit)
+            + fo_ref[0, at, :] * spread(fresh_share * inverse, head_dim, unit)
+        )
+    out_ref[...] = jnp.concatenate(outs, axis=0).astype(jnp.bfloat16)
+
+
+def finish(core, mine, other, fresh_sum, fresh_stats, unit, scale2):
+    half = mine.shape[0]
+    heads, tok_dev, head_dim = fresh_sum.shape
+    part = pl.BlockSpec((1,) + mine.shape[1:], lambda h, *_: (h % half, 0, 0))
+    own = lambda x: pl.BlockSpec((1,) + x.shape[1:], lambda h, *_: (h, 0, 0))
+    return pl.pallas_call(
+        lambda *refs: finish_kernel(unit, half, scale2, *refs),
+        grid_spec=pltpu.PrefetchScalarGridSpec(
+            num_scalar_prefetch=1,
+            grid=(heads,),
+            in_specs=[part, part, own(fresh_sum), own(fresh_stats)],
+            out_specs=pl.BlockSpec((tok_dev, head_dim), lambda h, *_: (0, h)),
+        ),
+        out_shape=jax.ShapeDtypeStruct((tok_dev, heads * head_dim), jnp.bfloat16),
+        name="finish",
+    )(core[None], mine, other, fresh_sum, fresh_stats)
+
+
+def compose_kernel(at_ref, *refs):
+    out_ref = refs[-1]
+    for k, ref in enumerate(refs[:-1]):
+
+        @pl.when(pl.program_id(1) == k)
+        def _(ref=ref):
+            out_ref[...] = ref[...]
+
+
+def compose(arrays, side):
+    line = arrays[0].shape[0]
+    block = (1,) + arrays[0].shape[1:]
+    zeros = (0,) * (len(block) - 1)
+    out = pl.pallas_call(
+        compose_kernel,
+        grid_spec=pltpu.PrefetchScalarGridSpec(
+            num_scalar_prefetch=1,
+            grid=(line, 4),
+            in_specs=[pl.BlockSpec(block, lambda z, k, at: (z,) + zeros)] * 4,
+            out_specs=pl.BlockSpec(block, lambda z, k, at: (z * 4 + (k ^ at[0]),) + zeros),
+        ),
+        out_shape=jax.ShapeDtypeStruct((line * 4,) + block[1:], arrays[0].dtype),
+        compiler_params=pltpu.CompilerParams(vmem_limit_bytes=40 * 2**20),
+        name="compose",
+    )(side[None], *arrays)
+    return out.reshape((-1,) + block[2:])
+
+
+def project_kernel(groups, at_ref, *refs):
+    att_refs, w_refs, (bias_ref, out_ref) = refs[:groups], refs[groups:-2], refs[-2:]
+    for k in range(4):
+
+        @pl.when(pl.program_id(1) == k)
+        def _(k=k):
+            total = bias_ref[...].reshape(1, -1)
+            for s in range(groups):
+                total = total + jnp.dot(
+                    att_refs[s][...],
+                    w_refs[k * groups + s][0],
+                    preferred_element_type=jnp.float32,
+                )
+            out_ref[...] = total.astype(jnp.bfloat16).reshape(out_ref.shape)
+
+
+def project(attended, weights, bias, side, group_at):
+    groups = len(attended)
+    tok_dev = attended[0].shape[0]
+    line, feats, cols = weights[0].shape
+    share = line // groups
+    blocks = share * 4
+    wide = cols % 128 == 0
+    place = lambda j, k, at: j * 4 + (k ^ at[0])
+
+    def weight_spec(s):
+        return pl.BlockSpec(
+            (1, feats, cols),
+            lambda j, k, at: (lax.rem(at[1] + groups - s, groups) * share + j, 0, 0),
+        )
+
+    if wide:
+        out_spec = pl.BlockSpec((tok_dev, cols), lambda j, k, at: (0, place(j, k, at)))
+        out_shape = (tok_dev, blocks * cols)
+    else:
+        out_spec = pl.BlockSpec((1, tok_dev, cols), lambda j, k, at: (place(j, k, at), 0, 0))
+        out_shape = (blocks, tok_dev, cols)
+    out = pl.pallas_call(
+        lambda *refs: project_kernel(groups, *refs),
+        grid_spec=pltpu.PrefetchScalarGridSpec(
+            num_scalar_prefetch=1,
+            grid=(share, 4),
+            in_specs=[pl.BlockSpec(x.shape, lambda j, k, at: (0, 0)) for x in attended]
+            + [weight_spec(s) for _ in range(4) for s in range(groups)]
+            + [pl.BlockSpec((1, 1, cols), lambda j, k, at: (place(j, k, at), 0, 0))],
+            out_specs=out_spec,
+        ),
+        out_shape=jax.ShapeDtypeStruct(out_shape, jnp.bfloat16),
+        compiler_params=pltpu.CompilerParams(vmem_limit_bytes=40 * 2**20),
+        name="project",
+    )(
+        jnp.stack([side, group_at]),
+        *attended,
+        *[w for w in weights for _ in range(groups)],
+        bias.reshape(blocks, 1, cols),
+    )
+    return out if wide else jnp.transpose(out, (1, 0, 2)).reshape(tok_dev, blocks * cols)
 
 
 def per_device(
@@ -419,12 +584,22 @@
     q_own = jnp.transpose(rotated_q, (1, 0, 2))
     q_mine, q_other = halves(q_own)
     q_places = gather_lines(in_order(q_mine, swap(q_other, 1), 1))
-    all_k = lax.all_gather(rotated_k, "pages", axis=0, tiled=True)
-    all_v = lax.all_gather(values, "pages", axis=0, tiled=True)
-    natural = Layout((0, 1, 2))
-    all_k = with_layout_constraint(all_k, natural)
-    all_v = with_layout_constraint(all_v, natural)
-    weight = lax.all_gather(out_weight, "pages", axis=1, tiled=True)
+    groups = lax.axis_size("heads")
+    group_at = lax.axis_index("heads")
+    share = page_devs // groups
+    moves = [
+        (i * page_devs + h * share + j, h * page_devs + i * share + j)
+        for i in range(groups)
+        for h in range(groups)
+        for j in range(share)
+    ]
+    weight_block = lax.ppermute(out_weight, ("heads", "pages"), moves)
+    side = device_at % 4
+    line_k, line_v, line_w = gather_line(rotated_k), gather_line(values), gather_line(weight_block)
+    q_blocks, line_k = lax.optimization_barrier(([q for q, _, _, _ in q_places], line_k))
+    all_k = compose(spread_across(line_k), side)
+    all_v = compose(spread_across(line_v), side)
+    weights = spread_across(line_w)
 
     my_slots = device_at * slot_count + jnp.arange(slot_count, dtype=jnp.int32)
     chip_slots = jnp.concatenate(
@@ -456,10 +631,11 @@
     k_heads = jnp.concatenate([k_mine, swap(k_other, 1)], axis=1)
     v_heads = jnp.concatenate([v_mine, swap(v_other, 1)], axis=1)
 
+    unit = math.gcd(span_len, tok_dev)
     line = page_devs // 4
     line_at, across = device_at // 4, (device_at // 2) % 2
     outs = cached_attention(
-        [q for q, _, _, _ in q_places],
+        q_blocks,
         [jnp.clip(at, 0, line - 1) * 2 + side for _, at, side, _ in q_places],
         [ok for _, _, _, ok in q_places],
         [((line_at + k) % line) * 2 + (across ^ d) for k in range(line) for d in range(2)],
@@ -469,57 +645,32 @@
         slot_starts,
         slot_counts,
         span_len,
+        unit,
         scale2,
     )
-    unit = math.gcd(span_len, chip_len)
     merged = lambda parts, ok: merge(parts, ok, chip_len, unit, scale2)
     chip_part = merge_lines([outs[2 * k : 2 * k + 2] for k in range(line)], merged)
     other_part = swap(chip_part, 1)
-    per_unit, units, _ = stat_rows_of(chip_len, unit)
-
-    def own_tokens(part):
-        rows = lax.dynamic_slice_in_dim(part[:, :chip_len], core * tok_dev, tok_dev, 1)
-        stats = part[:, chip_len : chip_len + 3 * units * per_unit].astype(jnp.float32)
-        stats = stats.reshape(half, 3, units, per_unit * 128)[..., :unit]
-        stats = stats.reshape(half, 3, chip_len)
-        stats = lax.dynamic_slice_in_dim(stats, core * tok_dev, tok_dev, 2)
-        return rows.astype(jnp.float32), stats[:, 0], stats[:, 1] + stats[:, 2]
-
-    cached_mean, cached_top, cached_total = [
-        in_order(mine, got, 0)
-        for mine, got in zip(own_tokens(chip_part), own_tokens(other_part))
-    ]
-
     window_at = jnp.minimum(request_ids[0], requests - 2) * span_len
     k_window = lax.dynamic_slice_in_dim(all_k, window_at, 2 * span_len, 0)
     v_window = lax.dynamic_slice_in_dim(all_v, window_at, 2 * span_len, 0)
     token_rows = jnp.stack([token_ids, request_ids * span_len])
     key_cols = (window_at + jnp.arange(2 * span_len, dtype=jnp.int32))[:, None]
-    fresh_sum, fresh_top, fresh_total = fresh_attention(
+    fresh_sum, fresh_stats = fresh_attention(
         q_own,
         jnp.transpose(k_window, (1, 0, 2)),
         jnp.transpose(v_window, (1, 2, 0)),
         token_rows,
         key_cols,
+        unit,
         scale2,
     )
-    fresh_sum = jnp.transpose(fresh_sum, (0, 2, 1))
-    fresh_top = fresh_top[:, 0]
-    fresh_total = fresh_total[:, 0]
-    best = jnp.maximum(cached_top, fresh_top)
-    cached_part = cached_total * jnp.exp2((cached_top - best) * scale2)
-    fresh_part = jnp.exp2((fresh_top - best) * scale2)
-    total = cached_part + fresh_total * fresh_part
-    attended = (
-        cached_mean * (cached_part / total)[..., None] + fresh_sum * (fresh_part / total)[..., None]
-    ).astype(jnp.bfloat16)
-    attended = jnp.transpose(attended, (1, 0, 2)).reshape(tok_dev, head_count * head_dim)
-
-    projected = jnp.dot(attended, weight, preferred_element_type=jnp.float32)
-    summed = lax.psum_scatter(
-        projected.astype(jnp.bfloat16), "heads", scatter_dimension=1, tiled=True
-    ).astype(jnp.float32)
-    hidden = (summed + out_bias[None, :]).astype(jnp.bfloat16)
+    attended = finish(core, chip_part, other_part, fresh_sum, fresh_stats, unit, scale2)
+    attended = [attended] + [
+        lax.ppermute(attended, "heads", [(h, (h + s) % groups) for h in range(groups)])
+        for s in range(1, groups)
+    ]
+    hidden = project(attended, weights, out_bias, side, group_at)
 
     page_shape = (requests * new_pages, PAGE, head_count, head_dim)
     key_out, value_out = write_pages(

time: 434 us -> 590 us (1.36)
  waiting for transfers between devices: 172 us -> 253 us
  starting transfers between devices: 45.3 us -> 95 us
  Pallas kernels: 102 us -> 138 us
  other arithmetic: 31.2 us -> 22.8 us
  matrix products: 7.87 us -> 0 us
  local copies, waits for them, and re-layouts: 59 us -> 65.1 us
    ppermute x9 -> x18, waiting for transfers between devices: 35.1 us -> 137 us  [swap(): return lax.ppermute(x, 'pages', [(p, p ^ bit) for p in range(devs)])]
    pallas_call x2 -> x6, Pallas kernels: 50.6 us -> 88.2 us  [the longest x1 34.6 us: cached_attention(): pl.pallas_call(lambda *refs: cached_kernel(unit, stat_unit, span, scale2,...]
    ppermute x12, starting transfers between devices: 30.1 us -> 62 us  [shift(): return lax.ppermute(x, 'pages', moves)]
    reduce_scatter x1 -> x0, waiting for transfers between devices: 22.4 us -> none  [per_device(): lax.psum_scatter(projected.astype(jnp.bfloat16), 'heads', scatter_dimensi...]
    ppermute x9 -> x18, starting transfers between devices: 4.84 us -> 14.2 us  [swap(): return lax.ppermute(x, 'pages', [(p, p ^ bit) for p in range(devs)])]
    pallas_call x0 -> x1, local copies, waits for them, and re-layouts: none -> 8.9 us  [compose(): pl.pallas_call(compose_kernel, grid_spec=pltpu.PrefetchScalarGridSpec(num...]
    dot_general x1 -> x0, matrix products: 7.87 us -> none  [per_device(): projected = jnp.dot(attended, weight, preferred_element_type=jnp.float32)]
    ppermute x0 -> x2, starting transfers between devices: none -> 7.33 us  [the longest x1 5.38 us: per_device(): weight_block = lax.ppermute(out_weight, ('heads', 'pages'), moves)]
  transfers between devices with their start and end apart: 31 -> 41, of which waited for: 13 -> 16; matrix products, arithmetic and copies ran while one was open for 16% -> 10% of each run, Pallas kernels for 23% -> 22%
where the time goes in v1:
time: 590 us; the launch traced here: 588 us
  waiting for transfers between devices  253 us (43%)
  Pallas kernels  138 us (23%)
  starting transfers between devices  95 us (16%)
  local copies, waits for them, and re-layouts  65.1 us (11%)
  other arithmetic  22.8 us (4%)
  between operations  14.9 us (3%)
    ppermute x18, waiting for transfers between devices, swap(): return lax.ppermute(x, 'pages', [(p, p ^ bit) for p in range(devs)])  137 us
    ppermute x12, waiting for transfers between devices, shift(): return lax.ppermute(x, 'pages', moves)  99 us
    ppermute x12, starting transfers between devices, shift(): return lax.ppermute(x, 'pages', moves)  62 us
    pallas_call x9, Pallas kernels, merge(): pl.pallas_call(lambda *refs: merge_kernel(unit, part_len, scale2, *refs),...  41.7 us
    unnamed x76, local copies, waits for them, and re-layouts  38.6 us
    pallas_call x1, Pallas kernels, cached_attention(): pl.pallas_call(lambda *refs: cached_kernel(unit, stat_unit, span, scale2,...  34.6 us
    pallas_call x2, Pallas kernels, compose(): pl.pallas_call(compose_kernel, grid_spec=pltpu.PrefetchScalarGridSpec(num...  24.3 us
    ppermute x18, starting transfers between devices, swap(): return lax.ppermute(x, 'pages', [(p, p ^ bit) for p in range(devs)])  14.2 us
  transfers between devices with their start and end apart: 41, of which 16 were waited for; matrix products, arithmetic and copies ran while one was open for 10% of the time, Pallas kernels for 22%

profile of v1, /device:TPU:12, one launch (start us, length us, event | category | flops | bytes accessed | tf_op | source)
XLA Modules:
  0.0 588.1 jit_solution(12466420015785304184)
XLA Ops:
  30.4 5.4 collective-permute-start.34
  35.8 7.3 %constant_dynamic-slice_fusion.2 = (bf16[12,128,4,128]{3,2,1,0:T(4,128)(2,1)}, bf16[12,128,4,128]{3,2,1,0:T(4,128)(2,1)}, bf16[12,128,4,128]{3,2,1,0:T(4,128)(2,1)S(1)}, bf16[12,128,4,128]{3,2,1,0:T(4,128)(2,1)}) fusion(bf16[12,128,8,128]{3,2,1,0:T(8,128)(2,1)S(1)} %copy-done, s32[]{:T(128)S(6)} %select_n.153, s32[]{:T(128)S(6)} %select_n.154, ...), kind=kLoop, calls=%fused_computation.53 | loop fusion | bytes 12582920 | tf_op jit(solution)/shard_map/dynamic-slice.4
  49.4 16.6 %collective-permute-done.2.refs_7_ = bf16[4,576,128]{2,1,0:T(8,128)(2,1)} collective-permute-done((bf16[4,576,128]{2,1,0:T(8,128)(2,1)}, bf16[4,576,128]{2,1,0:T(8,128)(2,1)}, u32[]{:S(2)}, u32[]{:S(2)}) %collective-permute-start.2) | collective-permute-done | bytes 589856 | tf_op jit(solution)/shard_map/ppermute | solution.py:275
  66.0 37.0 %collective-permute-start.6 = (bf16[4,576,128]{2,1,0:T(8,128)(2,1)}, bf16[4,576,128]{2,1,0:T(8,128)(2,1)}, u32[]{:S(2)}, u32[]{:S(2)}) collective-permute-start(bf16[4,576,128]{2,1,0:T(8,128)(2,1)} %collective-permute-done.2.refs_7_), channel_id=1, source_target_pairs={{4,8},{5,9},{6,10},{7,11},{8,12},{9,13},{10,14},{11,15},{20,24},{2... | collective-permute-start | bytes 1769480 | tf_op jit(solution)/shard_map/ppermute | solution.py:275
  108.5 36.0 %collective-permute-done.6.refs_11_ = bf16[4,576,128]{2,1,0:T(8,128)(2,1)} collective-permute-done((bf16[4,576,128]{2,1,0:T(8,128)(2,1)}, bf16[4,576,128]{2,1,0:T(8,128)(2,1)}, u32[]{:S(2)}, u32[]{:S(2)}) %collective-permute-start.6) | collective-permute-done | bytes 589856 | tf_op jit(solution)/shard_map/ppermute | solution.py:275
  146.0 5.2 collective-permute-done.8.refs_13_
  180.8 9.5 %collective-permute-done.9.refs_14_ = bf16[4,576,128]{2,1,0:T(8,128)(2,1)S(1)} collective-permute-done((bf16[4,576,128]{2,1,0:T(8,128)(2,1)}, bf16[4,576,128]{2,1,0:T(8,128)(2,1)S(1)}, u32[]{:S(2)}, u32[]{:S(2)}) %collective-permute-start.9) | collective-permute-done | bytes 589856 | tf_op jit(solution)/shard_map/ppermute | solution.py:308
  198.2 34.6 %cached_attention.1 = (bf16[4,608,128]{2,1,0:T(8,128)(2,1)S(1)}, bf16[4,608,128]{2,1,0:T(8,128)(2,1)}, bf16[4,608,128]{2,1,0:T(8,128)(2,1)S(1)}, bf16[4,608,128]...) custom-call(s32[22]{0:T(128)S(1)} %stack.197.refs_0_, ...), custom_call_target="tpu_custom_call" | custom-call | tf_op jit(solution)/shard_map/cached_attention/pallas_call | solution.py:154
  245.2 11.2 %collective-permute-done.19.refs_2_ = bf16[4,608,128]{2,1,0:T(8,128)(2,1)} collective-permute-done((bf16[4,608,128]{2,1,0:T(8,128)(2,1)}, bf16[4,608,128]{2,1,0:T(8,128)(2,1)}, u32[]{:S(2)}, u32[]{:S(2)}) %collective-permute-start.19) | collective-permute-done | bytes 622624 | tf_op jit(solution)/shard_map/ppermute | solution.py:269
  263.0 6.7 %collective-permute-done.17.refs_2_ = bf16[4,608,128]{2,1,0:T(8,128)(2,1)} collective-permute-done((bf16[4,608,128]{2,1,0:T(8,128)(2,1)}, bf16[4,608,128]{2,1,0:T(8,128)(2,1)}, u32[]{:S(2)}, u32[]{:S(2)}) %collective-permute-start.17) | collective-permute-done | bytes 622624 | tf_op jit(solution)/shard_map/ppermute | solution.py:269
  275.8 7.3 %collective-permute-done.16.refs_2_ = bf16[4,608,128]{2,1,0:T(8,128)(2,1)} collective-permute-done((bf16[4,608,128]{2,1,0:T(8,128)(2,1)}, bf16[4,608,128]{2,1,0:T(8,128)(2,1)}, u32[]{:S(2)}, u32[]{:S(2)}) %collective-permute-start.16) | collective-permute-done | bytes 622624 | tf_op jit(solution)/shard_map/ppermute | solution.py:269
  284.6 110.2 %collective-permute-done.18.refs_2_ = bf16[4,608,128]{2,1,0:T(8,128)(2,1)} collective-permute-done((bf16[4,608,128]{2,1,0:T(8,128)(2,1)}, bf16[4,608,128]{2,1,0:T(8,128)(2,1)}, u32[]{:S(2)}, u32[]{:S(2)}) %collective-permute-start.18) | collective-permute-done | bytes 622624 | tf_op jit(solution)/shard_map/ppermute | solution.py:269
  413.7 11.1 %collective-permute-done.21.refs_2_ = bf16[4,608,128]{2,1,0:T(8,128)(2,1)} collective-permute-done((bf16[4,608,128]{2,1,0:T(8,128)(2,1)}, bf16[4,608,128]{2,1,0:T(8,128)(2,1)}, u32[]{:S(2)}, u32[]{:S(2)}) %collective-permute-start.21) | collective-permute-done | bytes 622624 | tf_op jit(solution)/shard_map/ppermute | solution.py:275
  426.2 16.1 %collective-permute-done.24.refs_2_ = bf16[4,608,128]{2,1,0:T(8,128)(2,1)} collective-permute-done((bf16[4,608,128]{2,1,0:T(8,128)(2,1)}, bf16[4,608,128]{2,1,0:T(8,128)(2,1)}, u32[]{:S(2)}, u32[]{:S(2)}) %collective-permute-start.24) | collective-permute-done | bytes 622624 | tf_op jit(solution)/shard_map/ppermute | solution.py:275
  459.3 11.5 %collective-permute-done.22.refs_2_ = bf16[4,608,128]{2,1,0:T(8,128)(2,1)} collective-permute-done((bf16[4,608,128]{2,1,0:T(8,128)(2,1)}, bf16[4,608,128]{2,1,0:T(8,128)(2,1)}, u32[]{:S(2)}, u32[]{:S(2)}) %collective-permute-start.22) | collective-permute-done | bytes 622624 | tf_op jit(solution)/shard_map/ppermute | solution.py:275
  483.2 5.0 merge.17.refs_1_
  488.7 12.5 %compose.2 = bf16[16,288,8,128]{3,2,1,0:T(8,128)(2,1)} custom-call(s32[1]{0:T(128)} %bitcast.at_ref, bf16[4,288,8,128]{3,2,1,0:T(8,128)(2,1)} %all-gather.6.cloned.1.call-done.refs_0_, bf16[4,288,8,128]{3,2,1,0:T(8,128)(2,1)} %collective-permute-done.27.refs_1_, bf16[4,288,8,128]{3,2,1,0:T(8,128)(2,1)} %collective-permute-done.28.refs_2_, ...), custom_call_target="tpu_custom_call" | custom-call | tf_op jit(solution)/shard_map/compose/pallas_call | solution.py:462
  501.2 8.9 %copy.68 = bf16[16,288,8,128]{3,1,0,2:T(8,128)(2,1)} copy(bf16[16,288,8,128]{3,2,1,0:T(8,128)(2,1)} %compose.2) | data formatting | bytes 18874368 | tf_op jit(solution)/shard_map/compose/pallas_call | solution.py:462
  511.7 11.8 %compose.3 = bf16[16,288,8,128]{3,2,1,0:T(8,128)(2,1)} custom-call(s32[1]{0:T(128)} %bitcast.at_ref, bf16[4,288,8,128]{3,2,1,0:T(8,128)(2,1)S(1)} %bitcast.73, bf16[4,288,8,128]{3,2,1,0:T(8,128)(2,1)} %collective-permute-done.30.refs_1_, bf16[4,288,8,128]{3,2,1,0:T(8,128)(2,1)} %collective-permute-done.31.refs_2_, ...), custom_call_target="tpu_custom_call" | custom-call | tf_op jit(solution)/shard_map/compose/pallas_call | solution.py:462
  526.7 4.9 copy.74
  534.8 13.5 %fresh_attention.1 = (f32[8,288,128]{2,1,0:T(8,128)S(1)}, f32[8,8,128]{2,1,0:T(8,128)S(1)}) custom-call(bf16[8,288,128]{2,1,0:T(8,128)(2,1)S(1)} %copy-done.6, bf16[8,1536,128]{2,1,0:T(8,128)(2,1)S(1)} %dynamic-slice_bitcast_fusion.refs_1_, bf16[8,128,1536]{2,1,0:T(8,128)(2,1)S(1)} %bitcast.66, s32[2,288]{1,0:T(2,128)S(1)} %pad_add_fusion.refs_3_, ...), custom_call_target="tpu_custom_call" | custom-call | tf_op jit(solution)/shard_map/fresh_attention/pallas_call | solution.py:370
  550.0 6.5 %finish.1.refs_1_ = bf16[288,1024]{1,0:T(8,128)(2,1)} custom-call(s32[1]{0:T(128)} %bitcast.2.refs_0_, bf16[4,608,128]{2,1,0:T(8,128)(2,1)} %merge.17.refs_1_, bf16[4,608,128]{2,1,0:T(8,128)(2,1)} %collective-permute-done.26.refs_2_, f32[8,288,128]{2,1,0:T(8,128)} %copy-done.8, f32[8,8,128]{2,1,0:T(8,128)} %copy-done.23), custom_call_target="tpu_custom_call" | custom-call | tf_op jit(solution)/shard_map/finish/pallas_call | solution.py:436
  560.8 7.8 %write_pages.1 = (bf16[12,128,8,128]{3,2,1,0:T(8,128)(2,1)}, bf16[12,128,8,128]{3,2,1,0:T(8,128)(2,1)}) custom-call(s32[12]{0:T(128)S(1)} %convert_element_type.52.fresh_ref, s32[12]{0:T(128)S(1)} %fusion.4.index_ref, bf16[12,128,8,128]{3,2,1,0:T(8,128)(2,1)S(1)} %copy-done.1, bf16[12,128,8,128]{3,2,1,0:T(8,128)(2,1)S(1)} %copy-done, ...), custom_call_target="tpu_custom_call" | custom-call | tf_op jit(solution)/shard_map/write_pages/pallas_call | solution.py:253
  572.2 9.4 %project.1 = bf16[288,2048]{1,0:T(8,128)(2,1)} custom-call(s32[2]{0:T(128)S(1)} %pad_add_fusion.4.refs_0_, bf16[288,1024]{1,0:T(8,128)(2,1)S(1)} %copy-done.5, bf16[288,1024]{1,0:T(8,128)(2,1)} %collective-permute-done.33.refs_2_, bf16[4,1024,256]{2,1,0:T(8,128)(2,1)S(1)} %bitcast.69, bf16[4,1024,256]{2,1,0:T(8,128)(2,1)S(1)} %bitcast.70, ...), custom_call_target="tpu_custom_call" | custom-call | tf_op jit(solution)/shard_map/project/pallas_call | solution.py:514
  (206 shorter events, 167.4 us)
Async XLA Ops:
  7.2 185.7 %all-gather.6.cloned.1.call-start = ((), (), s32[]{:S(2)}) async-start(), calls=%async_computation | async-start | bytes 2949120 | tf_op jit(solution)/shard_map/all_gather | solution.py:281
  14.9 228.3 %all-gather.8.cloned.1.call-start = ((), (), s32[]{:S(2)}) async-start(), calls=%async_computation.1 | async-start | bytes 2949120 | tf_op jit(solution)/shard_map/all_gather | solution.py:281
  15.6 379.2 %all-gather.10.cloned.1.call-start = ((), (), s32[]{:S(2)}) async-start(), calls=%async_computation.2 | async-start | bytes 2621440 | tf_op jit(solution)/shard_map/all_gather | solution.py:281
  23.7 42.3 %collective-permute-start.2 = (bf16[4,576,128]{2,1,0:T(8,128)(2,1)}, bf16[4,576,128]{2,1,0:T(8,128)(2,1)}, u32[]{:S(2)}, u32[]{:S(2)}) collective-permute-start(bf16[4,576,128]{2,1,0:T(8,128)(2,1)} %maximum_select_fusion.refs_5_), channel_id=1, source_target_pairs={{0,4},{1,5},{2,6},{3,7},{4,8},{5,9},{6,10},{7,11},{8,12},{9,13},{1... | collective-permute-start | bytes 1769480 | tf_op jit(solution)/shard_map/ppermute | solution.py:275
  27.2 75.8 %collective-permute-start.4 = (bf16[4,576,128]{2,1,0:T(8,128)(2,1)}, bf16[4,576,128]{2,1,0:T(8,128)(2,1)}, u32[]{:S(2)}, u32[]{:S(2)}) collective-permute-start(bf16[4,576,128]{2,1,0:T(8,128)(2,1)} %maximum_select_fusion.refs_5_), channel_id=1, source_target_pairs={{4,0},{5,1},{6,2},{7,3},{8,4},{9,5},{10,6},{11,7},{12,8},{13,9},{1... | collective-permute-start | bytes 1769480 | tf_op jit(solution)/shard_map/ppermute | solution.py:275
  44.7 119.3 %collective-permute-start.14 = (bf16[4,12,128,128]{3,2,1,0:T(8,128)(2,1)}, bf16[4,12,128,128]{3,2,1,0:T(8,128)(2,1)}, u32[]{:S(2)}, u32[]{:S(2)}) collective-permute-start(bf16[4,12,128,128]{3,2,1,0:T(8,128)(2,1)} %bitcast.64), channel_id=1, source_target_pairs={{0,1},{1,0},{2,3},{3,2},{4,5},{5,4},{6,7},{7,6},{8,9},{9,8},{10,11... | collective-permute-start | bytes 4718600 | tf_op jit(solution)/shard_map/ppermute | solution.py:269
  48.4 116.3 %collective-permute-start.15 = (bf16[4,12,128,128]{3,2,1,0:T(8,128)(2,1)}, bf16[4,12,128,128]{3,2,1,0:T(8,128)(2,1)}, u32[]{:S(2)}, u32[]{:S(2)}) collective-permute-start(bf16[4,12,128,128]{3,2,1,0:T(8,128)(2,1)} %bitcast.81), channel_id=1, source_target_pairs={{0,1},{1,0},{2,3},{3,2},{4,5},{5,4},{6,7},{7,6},{8,9},{9,8},{10,11... | collective-permute-start | bytes 4718600 | tf_op jit(solution)/shard_map/ppermute | solution.py:269
  48.9 56.2 %collective-permute-start.1 = (bf16[4,576,128]{2,1,0:T(8,128)(2,1)}, bf16[4,576,128]{2,1,0:T(8,128)(2,1)}, u32[]{:S(2)}, u32[]{:S(2)}) collective-permute-start(bf16[4,576,128]{2,1,0:T(8,128)(2,1)} %maximum_select_fusion.refs_5_), channel_id=1, source_target_pairs={{0,2},{1,3},{2,0},{3,1},{4,6},{5,7},{6,4},{7,5},{8,10},{9,11},{10,... | collective-permute-start | bytes 1769480 | tf_op jit(solution)/shard_map/ppermute | solution.py:269
  66.0 78.5 %collective-permute-start.6 = (bf16[4,576,128]{2,1,0:T(8,128)(2,1)}, bf16[4,576,128]{2,1,0:T(8,128)(2,1)}, u32[]{:S(2)}, u32[]{:S(2)}) collective-permute-start(bf16[4,576,128]{2,1,0:T(8,128)(2,1)} %collective-permute-done.2.refs_7_), channel_id=1, source_target_pairs={{4,8},{5,9},{6,10},{7,11},{8,12},{9,13},{10,14},{11,15},{20,24},{2... | collective-permute-start | bytes 1769480 | tf_op jit(solution)/shard_map/ppermute | solution.py:275
  103.0 48.2 %collective-permute-start.8 = (bf16[4,576,128]{2,1,0:T(8,128)(2,1)}, bf16[4,576,128]{2,1,0:T(8,128)(2,1)}, u32[]{:S(2)}, u32[]{:S(2)}) collective-permute-start(bf16[4,576,128]{2,1,0:T(8,128)(2,1)} %collective-permute-done.4.refs_9_), channel_id=1, source_target_pairs={{4,0},{5,1},{6,2},{7,3},{8,4},{9,5},{10,6},{11,7},{20,16},{21,17},... | collective-permute-start | bytes 1769480 | tf_op jit(solution)/shard_map/ppermute | solution.py:275
  105.1 55.7 %collective-permute-start.3 = (bf16[4,576,128]{2,1,0:T(8,128)(2,1)}, bf16[4,576,128]{2,1,0:T(8,128)(2,1)}, u32[]{:S(2)}, u32[]{:S(2)}) collective-permute-start(bf16[4,576,128]{2,1,0:T(8,128)(2,1)} %collective-permute-done.2.refs_7_), channel_id=1, source_target_pairs={{4,6},{5,7},{6,4},{7,5},{8,10},{9,11},{10,8},{11,9},{12,14},{13,15... | collective-permute-start | bytes 1769480 | tf_op jit(solution)/shard_map/ppermute | solution.py:306
  243.2 182.9 %collective-permute-start.28 = (bf16[4,288,8,128]{3,2,1,0:T(8,128)(2,1)}, bf16[4,288,8,128]{3,2,1,0:T(8,128)(2,1)}, u32[]{:S(2)}, u32[]{:S(2)}) collective-permute-start(bf16[4,288,8,128]{3,2,1,0:T(8,128)(2,1)} %all-gather.6.cloned.1.call-done.refs_0_), channel_id=1, source_target_pairs={{0,2},{1,3},{2,0},{3,1},{4,6},{5,7},{6,4},{7,5},{8,10},{9,11},{10,... | collective-permute-start | bytes 7077896 | tf_op jit(solution)/shard_map/ppermute | solution.py:269
  243.2 199.0 %collective-permute-start.31 = (bf16[4,288,8,128]{3,2,1,0:T(8,128)(2,1)}, bf16[4,288,8,128]{3,2,1,0:T(8,128)(2,1)}, u32[]{:S(2)}, u32[]{:S(2)}) collective-permute-start(bf16[4,288,8,128]{3,2,1,0:T(8,128)(2,1)} %bitcast.71), channel_id=1, source_target_pairs={{0,2},{1,3},{2,0},{3,1},{4,6},{5,7},{6,4},{7,5},{8,10},{9,11},{10,... | collective-permute-start | bytes 7077896 | tf_op jit(solution)/shard_map/ppermute | solution.py:269
  256.4 138.4 %collective-permute-start.18 = (bf16[4,608,128]{2,1,0:T(8,128)(2,1)}, bf16[4,608,128]{2,1,0:T(8,128)(2,1)}, u32[]{:S(2)}, u32[]{:S(2)}) collective-permute-start(bf16[4,608,128]{2,1,0:T(8,128)(2,1)} %copy-done.25), channel_id=1, source_target_pairs={{0,2},{1,3},{2,0},{3,1},{4,6},{5,7},{6,4},{7,5},{8,10},{9,11},{10,... | collective-permute-start | bytes 1867784 | tf_op jit(solution)/shard_map/ppermute | solution.py:269
  269.7 125.1 %collective-permute-start.20 = (bf16[4,608,128]{2,1,0:T(8,128)(2,1)}, bf16[4,608,128]{2,1,0:T(8,128)(2,1)}, u32[]{:S(2)}, u32[]{:S(2)}) collective-permute-start(bf16[4,608,128]{2,1,0:T(8,128)(2,1)} %merge.12.refs_1_), channel_id=1, source_target_pairs={{0,4},{1,5},{2,6},{3,7},{16,20},{17,21},{18,22},{19,23}} | collective-permute-start | bytes 1867784 | tf_op jit(solution)/shard_map/ppermute | solution.py:275
  283.1 123.4 %collective-permute-start.23 = (bf16[4,608,128]{2,1,0:T(8,128)(2,1)}, bf16[4,608,128]{2,1,0:T(8,128)(2,1)}, u32[]{:S(2)}, u32[]{:S(2)}) collective-permute-start(bf16[4,608,128]{2,1,0:T(8,128)(2,1)} %merge.10.refs_1_), channel_id=1, source_target_pairs={{12,8},{13,9},{14,10},{15,11},{28,24},{29,25},{30,26},{31,27}} | collective-permute-start | bytes 1867784 | tf_op jit(solution)/shard_map/ppermute | solution.py:275
  394.8 60.3 %collective-permute-start.27 = (bf16[4,288,8,128]{3,2,1,0:T(8,128)(2,1)}, bf16[4,288,8,128]{3,2,1,0:T(8,128)(2,1)}, u32[]{:S(2)}, u32[]{:S(2)}) collective-permute-start(bf16[4,288,8,128]{3,2,1,0:T(8,128)(2,1)} %all-gather.6.cloned.1.call-done.refs_0_), channel_id=1, source_target_pairs={{0,1},{1,0},{2,3},{3,2},{4,5},{5,4},{6,7},{7,6},{8,9},{9,8},{10,11... | collective-permute-start | bytes 7077896 | tf_op jit(solution)/shard_map/ppermute | solution.py:269
  394.8 57.8 %collective-permute-start.36 = (bf16[4,1024,256]{2,1,0:T(8,128)(2,1)}, bf16[4,1024,256]{2,1,0:T(8,128)(2,1)}, u32[]{:S(2)}, u32[]{:S(2)}) collective-permute-start(bf16[4,1024,256]{2,1,0:T(8,128)(2,1)} %bitcast.67), channel_id=1, source_target_pairs={{0,2},{1,3},{2,0},{3,1},{4,6},{5,7},{6,4},{7,5},{8,10},{9,11},{10,... | collective-permute-start | bytes 6291464 | tf_op jit(solution)/shard_map/ppermute | solution.py:269
  426.1 62.1 %collective-permute-start.29 = (bf16[4,288,8,128]{3,2,1,0:T(8,128)(2,1)}, bf16[4,288,8,128]{3,2,1,0:T(8,128)(2,1)}, u32[]{:S(2)}, u32[]{:S(2)}) collective-permute-start(bf16[4,288,8,128]{3,2,1,0:T(8,128)(2,1)} %collective-permute-done.28.refs_2_), channel_id=1, source_target_pairs={{0,1},{1,0},{2,3},{3,2},{4,5},{5,4},{6,7},{7,6},{8,9},{9,8},{10,11... | collective-permute-start | bytes 7077896 | tf_op jit(solution)/shard_map/ppermute | solution.py:269
  442.2 67.8 %collective-permute-start.30 = (bf16[4,288,8,128]{3,2,1,0:T(8,128)(2,1)}, bf16[4,288,8,128]{3,2,1,0:T(8,128)(2,1)}, u32[]{:S(2)}, u32[]{:S(2)}) collective-permute-start(bf16[4,288,8,128]{3,2,1,0:T(8,128)(2,1)} %bitcast.72), channel_id=1, source_target_pairs={{0,1},{1,0},{2,3},{3,2},{4,5},{5,4},{6,7},{7,6},{8,9},{9,8},{10,11... | collective-permute-start | bytes 7077896 | tf_op jit(solution)/shard_map/ppermute | solution.py:269
  442.2 67.8 %collective-permute-start.32 = (bf16[4,288,8,128]{3,2,1,0:T(8,128)(2,1)}, bf16[4,288,8,128]{3,2,1,0:T(8,128)(2,1)}, u32[]{:S(2)}, u32[]{:S(2)}) collective-permute-start(bf16[4,288,8,128]{3,2,1,0:T(8,128)(2,1)} %collective-permute-done.31.refs_2_), channel_id=1, source_target_pairs={{0,1},{1,0},{2,3},{3,2},{4,5},{5,4},{6,7},{7,6},{8,9},{9,8},{10,11... | collective-permute-start | bytes 7077896 | tf_op jit(solution)/shard_map/ppermute | solution.py:269
  470.7 97.9 %collective-permute-start.35 = (bf16[4,1024,256]{2,1,0:T(8,128)(2,1)}, bf16[4,1024,256]{2,1,0:T(8,128)(2,1)}, u32[]{:S(2)}, u32[]{:S(2)}) collective-permute-start(bf16[4,1024,256]{2,1,0:T(8,128)(2,1)} %bitcast.68), channel_id=1, source_target_pairs={{0,1},{1,0},{2,3},{3,2},{4,5},{5,4},{6,7},{7,6},{8,9},{9,8},{10,11... | collective-permute-start | bytes 6291464 | tf_op jit(solution)/shard_map/ppermute | solution.py:269
  473.0 95.6 %collective-permute-start.37 = (bf16[4,1024,256]{2,1,0:T(8,128)(2,1)}, bf16[4,1024,256]{2,1,0:T(8,128)(2,1)}, u32[]{:S(2)}, u32[]{:S(2)}) collective-permute-start(bf16[4,1024,256]{2,1,0:T(8,128)(2,1)} %collective-permute-done.36.refs_7_.refs_8_), channel_id=1, source_target_pairs={{0,1},{1,0},{2,3},{3,2},{4,5},{5,4},{6,7},{7,6},{8,9},{9,8},{10,11... | collective-permute-start | bytes 6291464 | tf_op jit(solution)/shard_map/ppermute | solution.py:269
  488.1 61.8 %collective-permute-start.26 = (bf16[4,608,128]{2,1,0:T(8,128)(2,1)}, bf16[4,608,128]{2,1,0:T(8,128)(2,1)}, u32[]{:S(2)}, u32[]{:S(2)}) collective-permute-start(bf16[4,608,128]{2,1,0:T(8,128)(2,1)} %merge.17.refs_1_), channel_id=1, source_target_pairs={{0,1},{1,0},{2,3},{3,2},{4,5},{5,4},{6,7},{7,6},{8,9},{9,8},{10,11... | collective-permute-start | bytes 1867784 | tf_op jit(solution)/shard_map/ppermute | solution.py:269
  (52 other events, 569.0 us)
Sparse Core Ops, SparseCore 0:
  15.0 73.4 all-gather.5
  90.1 64.7 all-gather.7
  156.5 48.4 all-gather.9
